TPU v7x, 512 devices: a whole 4x4x16 slice. The times are simulated.
512 devices in a mesh: img: 16 (over x, y), tile: 32 (over z, core).
Axes of the slice: x: 4, y: 4, z: 16, core: 2. Of those that a mesh axis runs over, the one named last changes fastest.
Arguments:
- coarse: bfloat16 [65536, 1536], P(('img', 'tile')), parts along dimension 0, may hold values from -6 to 6
- fine_embed: bfloat16 [262144, 1536], P(('img', 'tile')), parts along dimension 0, may hold values from -6 to 6
- fine_gain: float32 [1536], replicated, may hold values from 0.1 to 1.9
- coarse_gain: float32 [1536], replicated, may hold values from 0.1 to 1.9
- w_query: bfloat16 [1536, 768], P('tile'), may hold values from -120 to 120
- w_kv: bfloat16 [1536, 1536], P('tile'), may hold values from -0.15625 to 0.15625
- w_out: bfloat16 [768, 1536], P('tile'), may hold values from -1.75 to 1.75
- readers: int32 [512, 16], P('img'), parts along dimension 0, may hold values from 0 to 31, all different within a row
- picks: int32 [512, 16], P('img'), parts along dimension 0, may hold values from 0 to 7
Outputs:
- attended: bfloat16 [262144, 1536], P(('img', 'tile')), parts along dimension 0
There are 16 independent parts, one for each index of `img`. A program takes and returns all parts, laid end to end along the dimension named above; an argument that names none is the same for every part. Nothing has to cross between parts.
Inputs may be any that keep to these rules, and one draw needn't show every extreme that they name: `readers`: row t names 16 different strips; every strip is named by some tile.
All inputs are finite; a program needn't handle non-finite values.
Results may differ from a plain program's by a relative error of at most 0.035.
The roundings to bfloat16 on the way count: a program that leaves them out, or rounds other values in their place, can miss the bound.
Values may be sent and summed in bfloat16 or wider, within the bound.
A program may use at most 64 MiB of HBM per device.

v0:
```python
import jax
import jax.numpy as jnp
from jax import lax
from jax.sharding import PartitionSpec as P

HEADS = 12
HDIM = 64
CW = 128
BLOCK = 16


EPSILON = 1e-06


def passed_along(value, axis, steps):
    count = lax.axis_size(axis)
    first, last = (max(0, -steps), min(count, count - steps))
    return lax.ppermute(value, axis, [(source, source + steps) for source in range(first, last)])


def normalize(values, gain_vector):
    widened = values.astype(jnp.float32)
    inverse = lax.rsqrt(jnp.mean(widened * widened, axis=-1, keepdims=True) + EPSILON)
    return widened * inverse * gain_vector


def attend(query, keyval):
    row_count = query.shape[0]
    key_count = keyval.shape[0]
    inner = HEADS * HDIM
    query_heads = query.reshape(row_count, HEADS, HDIM)
    key_heads = keyval[:, :inner].reshape(key_count, HEADS, HDIM)
    value_heads = keyval[:, inner:].reshape(key_count, HEADS, HDIM)
    scores = jnp.einsum(
        "qhd,khd->hqk", query_heads, key_heads, preferred_element_type=jnp.float32
    ) * HDIM ** (-0.5)
    maximum = jnp.max(scores, axis=-1, keepdims=True)
    exponent = jnp.exp(scores - maximum)
    weights = (exponent / jnp.sum(exponent, axis=-1, keepdims=True)).astype(jnp.bfloat16)
    mixed = jnp.einsum("hqk,khd->qhd", weights, value_heads, preferred_element_type=jnp.float32)
    return mixed.astype(jnp.bfloat16).reshape(row_count, inner)


def add_rows(left_rows, piece):
    return jnp.dot(left_rows, piece, preferred_element_type=jnp.float32)


def arrange_slots(blocks, readers, picks, my_index):
    matched = readers == my_index
    wanted = jnp.sum(jnp.where(matched, picks, 0), axis=1)
    present = jnp.any(matched, axis=1)
    chosen = jnp.take(blocks, wanted, axis=0)
    return jnp.where(present[:, None, None], chosen, jnp.zeros_like(chosen))


def collect(arrived, readers, my_index):
    own_reads = jnp.take(readers, my_index, axis=0)
    gathered = jnp.take(arrived, own_reads, axis=0)
    return gathered.reshape(-1, arrived.shape[2])


def body(coarse, fine_embed, fine_gain, coarse_gain, w_query, w_kv, w_out, readers, picks):
    model_width = coarse.shape[1]
    my_index = lax.axis_index("tile")
    group_slot = my_index % 8
    strip_rows = coarse.shape[0] // CW
    block_cols = CW // 8
    strip_blocks = coarse.reshape(strip_rows, 8, block_cols, model_width).transpose(1, 0, 2, 3)
    slot_ids = jnp.arange(8, dtype=jnp.int32)
    region = jnp.zeros_like(strip_blocks)
    for offset in range(-7, 8):
        if offset == 0:
            arrived = jnp.take(strip_blocks, group_slot, axis=0)
        else:
            target = group_slot + offset
            inside = (target >= 0) & (target < 8)
            outgoing = jnp.take(strip_blocks, jnp.clip(target, 0, 7), axis=0)
            outgoing = jnp.where(inside, outgoing, jnp.zeros_like(outgoing))
            arrived = passed_along(outgoing, "tile", offset)
        source = group_slot - offset
        region = jnp.where((slot_ids == source)[:, None, None, None], arrived[None], region)
    region = region.reshape(8 * strip_rows, block_cols, model_width)
    upsampled = jnp.repeat(jnp.repeat(region, 2, axis=0), 2, axis=1).reshape(-1, model_width)
    hidden = fine_embed.astype(jnp.float32) + upsampled.astype(jnp.float32)
    fine_normed = normalize(hidden, fine_gain).astype(jnp.bfloat16)
    coarse_normed = normalize(coarse, coarse_gain).astype(jnp.bfloat16)
    query_sum = add_rows(fine_normed, lax.all_gather(w_query, "tile", axis=0, tiled=True))
    kv_sum = add_rows(coarse_normed, lax.all_gather(w_kv, "tile", axis=0, tiled=True))
    query = query_sum.astype(jnp.bfloat16)
    keyval = kv_sum.astype(jnp.bfloat16)
    value_slots = arrange_slots(
        keyval.reshape(-1, BLOCK, keyval.shape[1]), readers, picks, my_index
    )
    value_arrived = lax.all_to_all(value_slots, "tile", split_axis=0, concat_axis=0, tiled=True)
    read_keyval = collect(value_arrived, readers, my_index)
    mixed = attend(query, read_keyval)
    out_sum = add_rows(mixed, lax.all_gather(w_out, "tile", axis=0, tiled=True))
    return out_sum.astype(jnp.bfloat16)


def solution(mesh):
    placed = (
        P(("img", "tile"), None),
        P(("img", "tile"), None),
        P(),
        P(),
        P("tile", None),
        P("tile", None),
        P("tile", None),
        P("img", None),
        P("img", None),
    )
    return jax.shard_map(
        body, mesh=mesh, in_specs=placed, out_specs=P(("img", "tile"), None), check_vma=False
    )
```

profile of v0, /device:TPU:1, one launch (start us, length us, event | category | flops | bytes accessed | tf_op | source)
XLA Modules:
  0.0 280.1 jit_solution(4166167376747194934)
XLA Ops:
  9.5 1.2 fusion.11
  10.6 79.4 %all-gather.4.cloned.1.call-done = bf16[1536,1536]{1,0:T(8,128)(2,1)} async-done(((bf16[48,1536]{1,0:T(8,128)(2,1)}), bf16[1536,1536]{1,0:T(8,128)(2,1)}) %all-gather.4.cloned.1.call-update) | async-done | bytes 4718608 | tf_op jit(solution)/shard_map/all_gather | solution.py:88
  90.1 3.3 %convolution_convert_fusion.1 = bf16[128,1536]{1,0:T(8,128)(2,1)S(1)} fusion(bf16[1536,1536]{1,0:T(8,128)(2,1)} %all-gather.4.cloned.1.call-done, bf16[128,1536]{1,0:T(8,128)(2,1)} %param.11, f32[1536]{0:T(1024)} %param.14, f32[128]{0:T(128)S(1)} %add_rsqrt_fusion.1), kind=kOutput, calls=%fused_computation.13 | convolution fusion | flops 604962816 | bytes 5511680 | tf_op jit(solution)/shard_map/dot_general | solution.py:45
  94.0 1.4 select_select_fusion
  95.5 8.2 %all-to-all-start = ((bf16[32,16,1536]{2,1,0:T(8,128)(2,1)}), bf16[32,16,1536]{2,1,0:T(8,128)(2,1)}, u32[]{:S(2)}, u32[]{:S(2)}) async-start(bf16[32,16,1536]{2,1,0:T(8,128)(2,1)} %select_select_fusion), calls=%async_computation | async-start | bytes 3145728 | tf_op jit(solution)/shard_map/all_to_all | solution.py:94
  103.9 5.1 %collective-permute-start.1 = (bf16[1,16,1536]{2,1,0:T(8,128)(2,1)S(1)}, bf16[1,16,1536]{2,1,0:T(8,128)(2,1)S(1)}, u32[]{:S(2)}, u32[]{:S(2)}) collective-permute-start(bf16[1,16,1536]{2,1,0:T(8,128)(2,1)S(1)} %get-tuple-element.38), channel_id=1, source_target_pairs={{0,6},{1,7},{2,8},{3,9},{4,10},{5,11},{6,12},{7,13},{8,14},{9,15},... | collective-permute-start | bytes 147464 | tf_op jit(solution)/shard_map/ppermute | solution.py:18
  109.0 5.2 %collective-permute-start.3 = (bf16[1,16,1536]{2,1,0:T(8,128)(2,1)S(1)}, bf16[1,16,1536]{2,1,0:T(8,128)(2,1)S(1)}, u32[]{:S(2)}, u32[]{:S(2)}) collective-permute-start(bf16[1,16,1536]{2,1,0:T(8,128)(2,1)S(1)} %get-tuple-element.43), channel_id=1, source_target_pairs={{0,4},{1,5},{2,6},{3,7},{4,8},{5,9},{6,10},{7,11},{8,12},{9,13},{1... | collective-permute-start | bytes 147464 | tf_op jit(solution)/shard_map/ppermute | solution.py:18
  114.2 4.8 %collective-permute-start.4 = (bf16[1,16,1536]{2,1,0:T(8,128)(2,1)S(1)}, bf16[1,16,1536]{2,1,0:T(8,128)(2,1)S(1)}, u32[]{:S(2)}, u32[]{:S(2)}) collective-permute-start(bf16[1,16,1536]{2,1,0:T(8,128)(2,1)S(1)} %get-tuple-element.42), channel_id=1, source_target_pairs={{0,3},{1,4},{2,5},{3,6},{4,7},{5,8},{6,9},{7,10},{8,11},{9,12},{10... | collective-permute-start | bytes 147464 | tf_op jit(solution)/shard_map/ppermute | solution.py:18
  119.0 4.3 %collective-permute-start.5 = (bf16[1,16,1536]{2,1,0:T(8,128)(2,1)S(1)}, bf16[1,16,1536]{2,1,0:T(8,128)(2,1)S(1)}, u32[]{:S(2)}, u32[]{:S(2)}) collective-permute-start(bf16[1,16,1536]{2,1,0:T(8,128)(2,1)S(1)} %get-tuple-element.41), channel_id=1, source_target_pairs={{0,2},{1,3},{2,4},{3,5},{4,6},{5,7},{6,8},{7,9},{8,10},{9,11},{10,... | collective-permute-start | bytes 147464 | tf_op jit(solution)/shard_map/ppermute | solution.py:18
  123.3 1.9 collective-permute-start.6
  125.9 52.0 %collective-permute-done.1 = bf16[1,16,1536]{2,1,0:T(8,128)(2,1)S(1)} collective-permute-done((bf16[1,16,1536]{2,1,0:T(8,128)(2,1)S(1)}, bf16[1,16,1536]{2,1,0:T(8,128)(2,1)S(1)}, u32[]{:S(2)}, u32[]{:S(2)}) %collective-permute-start.1) | collective-permute-done | bytes 49184 | tf_op jit(solution)/shard_map/ppermute | solution.py:18
  177.8 4.4 %collective-permute-start.7 = (bf16[1,16,1536]{2,1,0:T(8,128)(2,1)S(1)}, bf16[1,16,1536]{2,1,0:T(8,128)(2,1)S(1)}, u32[]{:S(2)}, u32[]{:S(2)}) collective-permute-start(bf16[1,16,1536]{2,1,0:T(8,128)(2,1)S(1)} %get-tuple-element.39), channel_id=1, source_target_pairs={{1,0},{2,1},{3,2},{4,3},{5,4},{6,5},{7,6},{8,7},{9,8},{10,9},{11,1... | collective-permute-start | bytes 147464 | tf_op jit(solution)/shard_map/ppermute | solution.py:18
  182.3 1.3 collective-permute-start.8
  183.9 1.3 collective-permute-start.9
  186.2 1.3 collective-permute-start.10
  187.9 1.3 collective-permute-start.11
  189.1 1.7 collective-permute-done.7
  190.9 1.3 collective-permute-start.12
  193.2 14.2 %collective-permute-start = (bf16[1,16,1536]{2,1,0:T(8,128)(2,1)S(1)}, bf16[1,16,1536]{2,1,0:T(8,128)(2,1)S(1)}, u32[]{:S(2)}, u32[]{:S(2)}) collective-permute-start(bf16[1,16,1536]{2,1,0:T(8,128)(2,1)S(1)} %get-tuple-element.32), channel_id=1, source_target_pairs={{0,7},{1,8},{2,9},{3,10},{4,11},{5,12},{6,13},{7,14},{8,15},{9,16}... | collective-permute-start | bytes 147464 | tf_op jit(solution)/shard_map/ppermute | solution.py:18
  207.3 5.1 %collective-permute-start.2 = (bf16[1,16,1536]{2,1,0:T(8,128)(2,1)S(1)}, bf16[1,16,1536]{2,1,0:T(8,128)(2,1)S(1)}, u32[]{:S(2)}, u32[]{:S(2)}) collective-permute-start(bf16[1,16,1536]{2,1,0:T(8,128)(2,1)S(1)} %bitcast_select_fusion.11), channel_id=1, source_target_pairs={{0,5},{1,6},{2,7},{3,8},{4,9},{5,10},{6,11},{7,12},{8,13},{9,14},{... | collective-permute-start | bytes 147464 | tf_op jit(solution)/shard_map/ppermute | solution.py:18
  212.5 1.5 collective-permute-start.13
  214.1 8.3 %collective-permute-done.13 = bf16[1,16,1536]{2,1,0:T(8,128)(2,1)S(1)} collective-permute-done((bf16[1,16,1536]{2,1,0:T(8,128)(2,1)S(1)}, bf16[1,16,1536]{2,1,0:T(8,128)(2,1)S(1)}, u32[]{:S(2)}, u32[]{:S(2)}) %collective-permute-start.13) | collective-permute-done | bytes 49184 | tf_op jit(solution)/shard_map/ppermute | solution.py:18
  223.2 2.8 %broadcast_in_dim.346 = f32[16,16,2,1536]{3,2,1,0:T(2,128)} broadcast(f32[16,16,1536]{2,1,0:T(8,128)S(1)} %bitcast.88), dimensions={0,1,3} | broadcast | bytes 4718592 | tf_op jit(solution)/shard_map/broadcast_in_dim | solution.py:83
  226.0 3.9 %convert_element_type.47 = f32[512,1536]{1,0:T(8,128)S(1)} reshape(f32[16,16,2,1536]{3,2,1,0:T(2,128)} %broadcast_in_dim.346) | data formatting | bytes 6291456 | tf_op jit(solution)/shard_map/convert_element_type | solution.py:84
  230.0 1.9 multiply_reduce_fusion.1
  231.9 4.6 %fusion.9 = bf16[512,768]{1,0:T(8,128)(2,1)} fusion(bf16[1536,768]{1,0:T(8,128)(2,1)} %all-gather.6.cloned.1.call-done, f32[512,1536]{1,0:T(8,128)S(1)} %convert_element_type.47, bf16[512,1536]{1,0:T(8,128)(2,1)} %param.12, f32[1536]{0:T(1024)S(1)} %copy-done.2, f32[512]{0:T(512)S(1)} %add_rsqrt_fusion), kind=kOutput, calls=%fused_computation.18 | convolution fusion | flops 1212284928 | bytes 7872512 | tf_op jit(solution)/shard_map/dot_general | solution.py:45
  236.5 1.4 copy.40
  237.9 2.0 gather_fusion.1
  240.4 4.8 %fusion.24 = (f32[12,512]{1,0:T(8,128)S(1)}, f32[12,512,256]{1,2,0:T(8,128)}) fusion(bf16[512,12,64]{0,2,1:T(8,128)(2,1)S(1)} %bitcast.96, bf16[256,12,64]{0,2,1:T(8,128)(2,1)S(1)} %bitcast.98), kind=kOutput, calls=%fused_computation.78 | convolution fusion | flops 206045440 | bytes 7495680 | tf_op jit(solution)/shard_map/sub | solution.py:38
  245.1 3.5 %fusion.10 = bf16[12,64,512]{2,1,0:T(8,128)(2,1)S(1)} fusion(bf16[256,12,64]{0,2,1:T(8,128)(2,1)S(1)} %bitcast.97, f32[12,512,256]{1,2,0:T(8,128)} %get-tuple-element.45, f32[12,512]{1,0:T(8,128)S(1)} %get-tuple-element.44), kind=kOutput, calls=%fused_computation.19 | convolution fusion | flops 204865536 | bytes 7495680 | tf_op jit(solution)/shard_map/hqk,khd->qhd/dot_general | solution.py:40
  248.6 20.8 %all-gather.8.cloned.1.call-done = bf16[768,1536]{1,0:T(8,128)(2,1)} async-done(((bf16[24,1536]{1,0:T(8,128)(2,1)}), bf16[768,1536]{1,0:T(8,128)(2,1)}) %all-gather.8.cloned.1.call-update) | async-done | bytes 2359312 | tf_op jit(solution)/shard_map/all_gather | solution.py:97
  269.4 4.2 %convolution_convert_fusion = bf16[512,1536]{1,0:T(8,128)(2,1)} fusion(bf16[512,768]{0,1:T(8,128)(2,1)S(1)} %bitcast.95, bf16[768,1536]{1,0:T(8,128)(2,1)} %all-gather.8.cloned.1.call-done), kind=kOutput, calls=%fused_computation.12 | convolution fusion | flops 1208745984 | bytes 4718592 | tf_op jit(solution)/shard_map/dot_general | solution.py:45
  (57 shorter events, 8.1 us)
Async XLA Ops:
  6.5 83.5 %all-gather.4.cloned.1.call-start = ((), (), s32[]{:S(2)}) async-start(), calls=%async_computation.1 | async-start | bytes 4866048 | tf_op jit(solution)/shard_map/all_gather | solution.py:88
  7.3 224.6 %all-gather.6.cloned.1.call-start = ((), (), s32[]{:S(2)}) async-start(), calls=%async_computation.2 | async-start | bytes 2433024 | tf_op jit(solution)/shard_map/all_gather | solution.py:87
  94.0 9.8 %copy-start = (bf16[128,1536]{1,0:T(8,128)(2,1)S(1)}, bf16[128,1536]{1,0:T(8,128)(2,1)}, u32[]{:S(2)}) copy-start(bf16[128,1536]{1,0:T(8,128)(2,1)} %param.11) | copy-start | bytes 1179652
  94.0 31.4 %copy-start.1 = (s32[32,16]{0,1:T(8,128)S(1)}, s32[32,16]{0,1:T(8,128)}, u32[]{:S(2)}) copy-start(s32[32,16]{0,1:T(8,128)} %param.18) | copy-start | bytes 6148
  95.5 142.4 %all-to-all-start = ((bf16[32,16,1536]{2,1,0:T(8,128)(2,1)}), bf16[32,16,1536]{2,1,0:T(8,128)(2,1)}, u32[]{:S(2)}, u32[]{:S(2)}) async-start(bf16[32,16,1536]{2,1,0:T(8,128)(2,1)} %select_select_fusion), calls=%async_computation | async-start | bytes 3145728 | tf_op jit(solution)/shard_map/all_to_all | solution.py:94
  103.7 165.7 %all-gather.8.cloned.1.call-start = ((), (), s32[]{:S(2)}) async-start(), calls=%async_computation.3 | async-start | bytes 2433024 | tf_op jit(solution)/shard_map/all_gather | solution.py:97
  103.9 74.0 %collective-permute-start.1 = (bf16[1,16,1536]{2,1,0:T(8,128)(2,1)S(1)}, bf16[1,16,1536]{2,1,0:T(8,128)(2,1)S(1)}, u32[]{:S(2)}, u32[]{:S(2)}) collective-permute-start(bf16[1,16,1536]{2,1,0:T(8,128)(2,1)S(1)} %get-tuple-element.38), channel_id=1, source_target_pairs={{0,6},{1,7},{2,8},{3,9},{4,10},{5,11},{6,12},{7,13},{8,14},{9,15},... | collective-permute-start | bytes 147464 | tf_op jit(solution)/shard_map/ppermute | solution.py:18
  109.0 73.3 %collective-permute-start.3 = (bf16[1,16,1536]{2,1,0:T(8,128)(2,1)S(1)}, bf16[1,16,1536]{2,1,0:T(8,128)(2,1)S(1)}, u32[]{:S(2)}, u32[]{:S(2)}) collective-permute-start(bf16[1,16,1536]{2,1,0:T(8,128)(2,1)S(1)} %get-tuple-element.43), channel_id=1, source_target_pairs={{0,4},{1,5},{2,6},{3,7},{4,8},{5,9},{6,10},{7,11},{8,12},{9,13},{1... | collective-permute-start | bytes 147464 | tf_op jit(solution)/shard_map/ppermute | solution.py:18
  114.2 69.7 %collective-permute-start.4 = (bf16[1,16,1536]{2,1,0:T(8,128)(2,1)S(1)}, bf16[1,16,1536]{2,1,0:T(8,128)(2,1)S(1)}, u32[]{:S(2)}, u32[]{:S(2)}) collective-permute-start(bf16[1,16,1536]{2,1,0:T(8,128)(2,1)S(1)} %get-tuple-element.42), channel_id=1, source_target_pairs={{0,3},{1,4},{2,5},{3,6},{4,7},{5,8},{6,9},{7,10},{8,11},{9,12},{10... | collective-permute-start | bytes 147464 | tf_op jit(solution)/shard_map/ppermute | solution.py:18
  119.0 67.2 %collective-permute-start.5 = (bf16[1,16,1536]{2,1,0:T(8,128)(2,1)S(1)}, bf16[1,16,1536]{2,1,0:T(8,128)(2,1)S(1)}, u32[]{:S(2)}, u32[]{:S(2)}) collective-permute-start(bf16[1,16,1536]{2,1,0:T(8,128)(2,1)S(1)} %get-tuple-element.41), channel_id=1, source_target_pairs={{0,2},{1,3},{2,4},{3,5},{4,6},{5,7},{6,8},{7,9},{8,10},{9,11},{10,... | collective-permute-start | bytes 147464 | tf_op jit(solution)/shard_map/ppermute | solution.py:18
  123.3 64.5 %collective-permute-start.6 = (bf16[1,16,1536]{2,1,0:T(8,128)(2,1)S(1)}, bf16[1,16,1536]{2,1,0:T(8,128)(2,1)S(1)}, u32[]{:S(2)}, u32[]{:S(2)}) collective-permute-start(bf16[1,16,1536]{2,1,0:T(8,128)(2,1)S(1)} %get-tuple-element.40), channel_id=1, source_target_pairs={{0,1},{1,2},{2,3},{3,4},{4,5},{5,6},{6,7},{7,8},{8,9},{9,10},{10,1... | collective-permute-start | bytes 147464 | tf_op jit(solution)/shard_map/ppermute | solution.py:18
  177.8 13.0 %collective-permute-start.7 = (bf16[1,16,1536]{2,1,0:T(8,128)(2,1)S(1)}, bf16[1,16,1536]{2,1,0:T(8,128)(2,1)S(1)}, u32[]{:S(2)}, u32[]{:S(2)}) collective-permute-start(bf16[1,16,1536]{2,1,0:T(8,128)(2,1)S(1)} %get-tuple-element.39), channel_id=1, source_target_pairs={{1,0},{2,1},{3,2},{4,3},{5,4},{6,5},{7,6},{8,7},{9,8},{10,9},{11,1... | collective-permute-start | bytes 147464 | tf_op jit(solution)/shard_map/ppermute | solution.py:18
  182.3 10.9 %collective-permute-start.8 = (bf16[1,16,1536]{2,1,0:T(8,128)(2,1)S(1)}, bf16[1,16,1536]{2,1,0:T(8,128)(2,1)S(1)}, u32[]{:S(2)}, u32[]{:S(2)}) collective-permute-start(bf16[1,16,1536]{2,1,0:T(8,128)(2,1)S(1)} %get-tuple-element.37), channel_id=1, source_target_pairs={{2,0},{3,1},{4,2},{5,3},{6,4},{7,5},{8,6},{9,7},{10,8},{11,9},{12,... | collective-permute-start | bytes 147464 | tf_op jit(solution)/shard_map/ppermute | solution.py:18
  183.9 23.5 %collective-permute-start.9 = (bf16[1,16,1536]{2,1,0:T(8,128)(2,1)S(1)}, bf16[1,16,1536]{2,1,0:T(8,128)(2,1)S(1)}, u32[]{:S(2)}, u32[]{:S(2)}) collective-permute-start(bf16[1,16,1536]{2,1,0:T(8,128)(2,1)S(1)} %get-tuple-element.36), channel_id=1, source_target_pairs={{3,0},{4,1},{5,2},{6,3},{7,4},{8,5},{9,6},{10,7},{11,8},{12,9},{13... | collective-permute-start | bytes 147464 | tf_op jit(solution)/shard_map/ppermute | solution.py:18
  186.2 26.3 %collective-permute-start.10 = (bf16[1,16,1536]{2,1,0:T(8,128)(2,1)S(1)}, bf16[1,16,1536]{2,1,0:T(8,128)(2,1)S(1)}, u32[]{:S(2)}, u32[]{:S(2)}) collective-permute-start(bf16[1,16,1536]{2,1,0:T(8,128)(2,1)S(1)} %get-tuple-element.35), channel_id=1, source_target_pairs={{4,0},{5,1},{6,2},{7,3},{8,4},{9,5},{10,6},{11,7},{12,8},{13,9},{1... | collective-permute-start | bytes 147464 | tf_op jit(solution)/shard_map/ppermute | solution.py:18
  187.9 26.3 %collective-permute-start.11 = (bf16[1,16,1536]{2,1,0:T(8,128)(2,1)S(1)}, bf16[1,16,1536]{2,1,0:T(8,128)(2,1)S(1)}, u32[]{:S(2)}, u32[]{:S(2)}) collective-permute-start(bf16[1,16,1536]{2,1,0:T(8,128)(2,1)S(1)} %get-tuple-element.34), channel_id=1, source_target_pairs={{5,0},{6,1},{7,2},{8,3},{9,4},{10,5},{11,6},{12,7},{13,8},{14,9},{... | collective-permute-start | bytes 147464 | tf_op jit(solution)/shard_map/ppermute | solution.py:18
  190.9 23.3 %collective-permute-start.12 = (bf16[1,16,1536]{2,1,0:T(8,128)(2,1)S(1)}, bf16[1,16,1536]{2,1,0:T(8,128)(2,1)S(1)}, u32[]{:S(2)}, u32[]{:S(2)}) collective-permute-start(bf16[1,16,1536]{2,1,0:T(8,128)(2,1)S(1)} %get-tuple-element.33), channel_id=1, source_target_pairs={{6,0},{7,1},{8,2},{9,3},{10,4},{11,5},{12,6},{13,7},{14,8},{15,9},... | collective-permute-start | bytes 147464 | tf_op jit(solution)/shard_map/ppermute | solution.py:18
  193.2 21.0 %collective-permute-start = (bf16[1,16,1536]{2,1,0:T(8,128)(2,1)S(1)}, bf16[1,16,1536]{2,1,0:T(8,128)(2,1)S(1)}, u32[]{:S(2)}, u32[]{:S(2)}) collective-permute-start(bf16[1,16,1536]{2,1,0:T(8,128)(2,1)S(1)} %get-tuple-element.32), channel_id=1, source_target_pairs={{0,7},{1,8},{2,9},{3,10},{4,11},{5,12},{6,13},{7,14},{8,15},{9,16}... | collective-permute-start | bytes 147464 | tf_op jit(solution)/shard_map/ppermute | solution.py:18
  207.3 6.8 %collective-permute-start.2 = (bf16[1,16,1536]{2,1,0:T(8,128)(2,1)S(1)}, bf16[1,16,1536]{2,1,0:T(8,128)(2,1)S(1)}, u32[]{:S(2)}, u32[]{:S(2)}) collective-permute-start(bf16[1,16,1536]{2,1,0:T(8,128)(2,1)S(1)} %bitcast_select_fusion.11), channel_id=1, source_target_pairs={{0,5},{1,6},{2,7},{3,8},{4,9},{5,10},{6,11},{7,12},{8,13},{9,14},{... | collective-permute-start | bytes 147464 | tf_op jit(solution)/shard_map/ppermute | solution.py:18
  212.5 10.0 %collective-permute-start.13 = (bf16[1,16,1536]{2,1,0:T(8,128)(2,1)S(1)}, bf16[1,16,1536]{2,1,0:T(8,128)(2,1)S(1)}, u32[]{:S(2)}, u32[]{:S(2)}) collective-permute-start(bf16[1,16,1536]{2,1,0:T(8,128)(2,1)S(1)} %bitcast_select_fusion), channel_id=1, source_target_pairs={{7,0},{8,1},{9,2},{10,3},{11,4},{12,5},{13,6},{14,7},{15,8},{16,9}... | collective-permute-start | bytes 147464 | tf_op jit(solution)/shard_map/ppermute | solution.py:18
  230.0 1.9 copy-start.2
Sparse Core Ops, SparseCore 0:
  9.5 80.5 all-gather.3
  92.2 101.5 all-gather.5
  195.9 73.3 all-gather.7
where the time goes:
time: 281 us; the launch traced here: 280 us
  waiting for transfers between devices  166 us (59%)
  starting transfers between devices  61.2 us (22%)
  matrix products  20.3 us (7%)
  between operations  13.7 us (5%)
  local copies, waits for them, and re-layouts  11.5 us (4%)
  other arithmetic  7 us (2%)
    all_gather x1, waiting for transfers between devices, body(): lax.all_gather(w_kv, 'tile', axis=0, tiled=True)  79.4 us
    ppermute x14, waiting for transfers between devices, passed_along(): lax.ppermute(value, axis, [(source, source + steps) for source in range(f...  64.7 us
    ppermute x14, starting transfers between devices, passed_along(): lax.ppermute(value, axis, [(source, source + steps) for source in range(f...  52.9 us
    all_gather x1, waiting for transfers between devices, body(): out_sum = add_rows(mixed, lax.all_gather(w_out, 'tile', axis=0, tiled=True))  20.8 us
    dot_general x3, matrix products, add_rows(): return jnp.dot(left_rows, piece, preferred_element_type=jnp.float32)  12.1 us
    all_to_all x1, starting transfers between devices, body(): lax.all_to_all(value_slots, 'tile', split_axis=0, concat_axis=0, tiled=True)  8.2 us
  transfers between devices with their start and end apart: 18, of which 9 were waited for; matrix products, arithmetic and copies ran while one was open for 12% of the time, Pallas kernels for 0%

commit v1 on v0

v1 whole, which is shorter than its diff:
```python
import functools

import jax
import jax.numpy as jnp
from jax import lax
from jax.experimental import pallas as pl
from jax.experimental.pallas import tpu as pltpu
from jax.sharding import PartitionSpec as P

HEADS = 12
HDIM = 64
BLOCK = 16
NZ = 16
NT = 32
D = 1536
HD = 768
LONG = 5
SHORT = 4
EPSILON = 1e-06
MESH = pl.DeviceIdType.MESH


def wrap(value, size):
    return lax.rem(value + size, size)


def gather_kernel(
    coarse_ref, shard_ref, blk_ref, w_ref, x_ref, up_ref,
    l1, l2, l3, l4, l5, s1, s2, s3, s4, stage, far_l, far_s, local_sem, zw_send, zw_recv,
    c_send, c_recv, far_send, far_recv, near_send, near_recv, up_send, up_recv,
    a_send, a_recv, b_send, b_recv, d_send, d_recv,
):
    img, tile = lax.axis_index("img"), lax.axis_index("tile")
    z, core = tile // 2, lax.rem(tile, 2)
    other = 1 - core
    sign = 1 - 2 * core
    gx, gy = img // 4, lax.rem(img, 4)
    a = jnp.where(core == 0, gx, gy)
    b = jnp.where(core == 0, gy, gx)

    def along(steps):
        return wrap(z + sign * steps, NZ)

    def on_z(steps, which):
        return {"img": img, "tile": along(steps) * 2 + which}

    def on_plane(first, second):
        first, second = wrap(first, 4), wrap(second, 4)
        return {"img": jnp.where(core == 0, first * 4 + second, second * 4 + first), "tile": tile}

    sibling = {"img": img, "tile": z * 2 + other}
    a_up, a_down = on_plane(a + 1, b), on_plane(a - 1, b)
    b_up, b_down = on_plane(a, b + 1), on_plane(a, b - 1)
    ahead, behind = on_z(1, core), on_z(-1, core)

    partners = [sibling, a_up, a_down, b_up, b_down]
    partners += [on_z(j, which) for j in (-3, -2, -1, 1, 2, 3) for which in (core, other)]
    barrier = pltpu.get_barrier_semaphore()
    for partner in partners:
        pl.semaphore_signal(barrier, inc=1, device_id=partner, device_id_type=MESH)
    pl.semaphore_wait(barrier, len(partners))

    def remote(src, dst, send, recv, device):
        return pltpu.make_async_remote_copy(
            src_ref=src, dst_ref=dst, send_sem=send, recv_sem=recv, device_id=device, device_id_type=MESH
        )

    pending = []

    def go(copy):
        copy.start()
        pending.append(copy)
        return copy

    bp = lax.rem(b, 2)

    def zw_copy(step, forward):
        source = along(-(step - 1) if forward else step - 1)
        where = w_ref.at[a, bp, :, source, core]
        src = shard_ref.at[a, bp] if step == 1 else where
        slot = step - 1 if forward else 8 + step - 1
        return remote(src, where, zw_send.at[slot], zw_recv.at[slot], ahead if forward else behind)

    long_buf = [coarse_ref, l1, l2, l3, l4, l5]
    short_buf = [coarse_ref, s1, s2, s3, s4]

    def c_copy(step, half, forward):
        bufs = long_buf if forward else short_buf
        slot = 2 * (step - 1 if forward else LONG + step - 1) + half
        part = pl.ds(4 * half, 4)
        return remote(
            bufs[step - 1].at[part], bufs[step].at[part], c_send.at[slot], c_recv.at[slot],
            ahead if forward else behind,
        )

    zw, cc = {}, {}

    def zw_start(step):
        zw[step, True] = go(zw_copy(step, True))
        if step <= 7:
            zw[step, False] = go(zw_copy(step, False))

    def zw_wait(step):
        zw[step, True].wait_recv()
        if step <= 7:
            zw[step, False].wait_recv()

    def c_start(step, half):
        if step <= LONG:
            cc[step, half, True] = go(c_copy(step, half, True))
        if step <= SHORT:
            cc[step, half, False] = go(c_copy(step, half, False))

    def c_wait(step, half):
        if step <= LONG:
            cc[step, half, True].wait_recv()
        if step <= SHORT:
            cc[step, half, False].wait_recv()

    conditional = []

    def share(buf, steps, index, distance):
        strip = along(steps) * 2 + core
        x_ref[core, distance] = buf[blk_ref[tile, strip]]
        stage[index] = buf[blk_ref[z * 2 + other, strip]]
        go(remote(stage.at[index], x_ref.at[core, distance], near_send.at[index], near_recv.at[index], sibling))
        if abs(steps) <= 3:
            position = lax.rem(z, 4) + sign * steps
            inside = (position >= 0) & (position < 4)
            column = lax.rem(tile, 8)
            column_other = lax.rem(z * 2 + other, 8)
            kept = jnp.clip(position, 0, 3)
            row = 2 * kept + core
            sent = remote(
                buf.at[column_other], up_ref.at[row], up_send.at[index], up_recv.at[kept], sibling
            )

            @pl.when(inside)
            def _():
                up_ref[row] = buf[column]
                sent.start()

            conditional.append((inside, sent))

    def share_step(step):
        if step == 0:
            share(coarse_ref, 0, 0, 0)
            return
        if step <= LONG:
            share(long_buf[step], -step, step, step)
        if step <= SHORT:
            share(short_buf[step], step, LONG + step, NZ - step)

    far = []

    def send_far(forward):
        buf = l5 if forward else s4
        held = LONG if forward else SHORT
        picked = far_l if forward else far_s
        strip = along(-LONG if forward else SHORT) * 2 + core
        for j in (3, 2, 1):
            target = along(j if forward else -j)
            distance = held + j if forward else NZ - held - j
            for e in range(2):
                which = core if e == 0 else other
                slot = (0 if forward else 6) + 2 * (j - 1) + e
                picked[2 * (j - 1) + e] = buf[blk_ref[target * 2 + which, strip]]
                far.append(go(remote(
                    picked.at[2 * (j - 1) + e], x_ref.at[core, distance], far_send.at[slot], far_recv.at[slot],
                    {"img": img, "tile": target * 2 + which},
                )))

    own = pltpu.make_async_copy(shard_ref.at[a, bp], w_ref.at[a, bp, :, z, core], local_sem)
    own.start()
    zw_start(1)
    c_start(1, 0)
    c_start(1, 1)
    share_step(0)
    for step in (2, 3, 4):
        zw_wait(step - 1)
        zw_start(step)
    c_wait(1, 0)
    c_start(2, 0)
    zw_wait(4)
    zw_start(5)
    c_wait(1, 1)
    c_start(2, 1)
    share_step(1)
    for step in (6, 7, 8):
        zw_wait(step - 1)
        zw_start(step)
    c_wait(2, 0)
    c_start(3, 0)
    c_wait(2, 1)
    c_start(3, 1)
    zw_wait(8)
    own.wait()

    def piece(position):
        return w_ref.at[wrap(position, 4), bp, :, :, core]

    def half_piece(position, half):
        return w_ref.at[wrap(position, 4), bp, :, pl.ds(8 * half, 8), core]

    a1 = go(remote(piece(a), piece(a), a_send.at[0], a_recv.at[0], a_up))
    a2 = go(remote(piece(a), piece(a), a_send.at[1], a_recv.at[1], a_down))
    share_step(2)
    c_wait(3, 0)
    c_start(4, 0)
    a1.wait_recv()
    a2.wait_recv()
    a3 = go(remote(half_piece(a - 1, 0), half_piece(a - 1, 0), a_send.at[2], a_recv.at[2], a_up))
    a4 = go(remote(half_piece(a + 1, 1), half_piece(a + 1, 1), a_send.at[3], a_recv.at[3], a_down))
    c_wait(3, 1)
    c_start(4, 1)
    share_step(3)
    a3.wait_recv()
    a4.wait_recv()

    b1 = go(remote(
        w_ref.at[:, bp, :, pl.ds(0, 8), core], w_ref.at[:, bp, :, pl.ds(0, 8), core], b_send.at[0], b_recv.at[0], b_up,
    ))
    b2 = go(remote(
        w_ref.at[:, bp, :, pl.ds(8, 8), core], w_ref.at[:, bp, :, pl.ds(8, 8), core], b_send.at[1], b_recv.at[1], b_down,
    ))
    d1 = go(remote(w_ref.at[:, bp, :, :, core], w_ref.at[:, bp, :, :, core], d_send.at[0], d_recv.at[0], sibling))
    c_wait(4, 0)
    c_start(5, 0)
    c_wait(4, 1)
    c_start(5, 1)
    send_far(False)
    share_step(4)
    c_wait(5, 0)
    c_wait(5, 1)
    send_far(True)
    share_step(5)
    b1.wait_recv()
    b2.wait_recv()
    d2 = go(remote(
        w_ref.at[:, 1 - bp, :, :, core], w_ref.at[:, 1 - bp, :, :, core], d_send.at[1], d_recv.at[1], sibling,
    ))
    for copy in far:
        copy.wait_recv()
    for index in range(LONG + SHORT + 1):
        remote(stage.at[index], x_ref.at[core, index], near_send.at[index], near_recv.at[index], sibling).wait_recv()
    for row in range(4):
        remote(coarse_ref.at[0], up_ref.at[row], up_send.at[row], up_recv.at[row], sibling).wait_recv()
    d1.wait_recv()
    d2.wait_recv()
    for copy in pending:
        copy.wait_send()
    for inside, copy in conditional:
        pl.when(inside)(copy.wait_send)


def gather(coarse, shard, blk):
    vmem = pl.BlockSpec(memory_space=pltpu.VMEM)
    strip = pltpu.VMEM((8, BLOCK, D), jnp.bfloat16)
    dma = pltpu.SemaphoreType.DMA
    near = LONG + SHORT + 1
    return pl.pallas_call(
        gather_kernel,
        out_shape=(
            jax.ShapeDtypeStruct((4, 2, 3, NZ, 2, 48, 128), jnp.bfloat16),
            jax.ShapeDtypeStruct((2, NZ, BLOCK, D), jnp.bfloat16),
            jax.ShapeDtypeStruct((8, BLOCK, D), jnp.bfloat16),
        ),
        in_specs=[vmem, vmem, pl.BlockSpec(memory_space=pltpu.SMEM)],
        out_specs=(vmem, vmem, vmem),
        scratch_shapes=[strip] * (LONG + SHORT) + [
            pltpu.VMEM((near, BLOCK, D), jnp.bfloat16),
            pltpu.VMEM((6, BLOCK, D), jnp.bfloat16),
            pltpu.VMEM((6, BLOCK, D), jnp.bfloat16),
            dma,
            dma((16,)), dma((16,)),
            dma((2 * (LONG + SHORT),)), dma((2 * (LONG + SHORT),)),
            dma((12,)), dma((12,)),
            dma((near,)), dma((near,)),
            dma((near,)), dma((4,)),
            dma((4,)), dma((4,)),
            dma((2,)), dma((2,)),
            dma((2,)), dma((2,)),
        ],
        compiler_params=pltpu.CompilerParams(
            collective_id=0, has_side_effects=True, vmem_limit_bytes=56 << 20
        ),
    )(coarse, shard, blk)


def normalized(values, gain):
    inverse = lax.rsqrt(jnp.mean(values * values, axis=-1, keepdims=True) + EPSILON)
    return (values * inverse * gain).astype(jnp.bfloat16)


def compute_kernel(
    slot_ref, fine_ref, up_ref, x_ref, w_ref, fine_gain_ref, coarse_gain_ref, out_ref,
    fine_n, coarse_n, query, keyval, mixed, w_out,
):
    rows = lax.broadcasted_iota(jnp.int32, (32, BLOCK), 0) // 2
    spread = (rows == lax.broadcasted_iota(jnp.int32, (32, BLOCK), 1)).astype(jnp.bfloat16)

    @pl.loop(0, 8)
    def _(i):
        up = jnp.dot(spread, up_ref[i], preferred_element_type=jnp.float32)
        for half in range(2):
            part = pl.ds(pl.multiple_of(i * 64 + half * 32, 32), 32)
            hidden = fine_ref[part, :].astype(jnp.float32) + up
            fine_n[part, :] = normalized(hidden, fine_gain_ref[...])

    @pl.loop(0, 16)
    def _(r):
        slot = slot_ref[r]
        values = x_ref[slot // NZ, lax.rem(slot, NZ)].astype(jnp.float32)
        coarse_n[pl.ds(pl.multiple_of(r * BLOCK, BLOCK), BLOCK), :] = normalized(values, coarse_gain_ref[...])

    def pair(first):
        return jnp.concatenate([w_ref[first].reshape(D, 128), w_ref[first + 1].reshape(D, 128)], axis=1)

    @pl.loop(0, 3)
    def _(j):
        query[:, pl.ds(pl.multiple_of(j * 256, 256), 256)] = jnp.dot(
            fine_n[...], pair(2 * j), preferred_element_type=jnp.float32
        ).astype(jnp.bfloat16)

    @pl.loop(0, 6)
    def _(j):
        keyval[:, pl.ds(pl.multiple_of(j * 256, 256), 256)] = jnp.dot(
            coarse_n[...], pair(6 + 2 * j), preferred_element_type=jnp.float32
        ).astype(jnp.bfloat16)

    @pl.loop(0, NZ)
    def _(k):
        for j in range(6):
            even = w_ref[18 + j, k, 0].astype(jnp.float32)
            odd = w_ref[18 + j, k, 1].astype(jnp.float32)
            part = pl.ds(pl.multiple_of(k * 48, 48), 48)
            for half in range(2):
                lanes = pl.ds((j + 6 * half) * 128, 128)
                cut = slice(24 * half, 24 * half + 24)
                w_out[part, lanes] = jnp.concatenate([even[cut], odd[cut]], axis=0).astype(jnp.bfloat16)

    @pl.loop(0, HEADS // 2)
    def _(p):
        lanes = pl.ds(pl.multiple_of(p * 128, 128), 128)
        value_lanes = pl.ds(pl.multiple_of(HD + p * 128, 128), 128)
        queries, keys, values = query[:, lanes], keyval[:, lanes], keyval[:, value_lanes]
        results = []
        for h in range(2):
            cut = slice(h * HDIM, h * HDIM + HDIM)
            scores = lax.dot_general(
                queries[:, cut], keys[:, cut], (((1,), (1,)), ((), ())), preferred_element_type=jnp.float32
            ) * HDIM ** (-0.5)
            exponent = jnp.exp(scores - jnp.max(scores, axis=-1, keepdims=True))
            weights = (exponent / jnp.sum(exponent, axis=-1, keepdims=True)).astype(jnp.bfloat16)
            results.append(jnp.dot(weights, values[:, cut], preferred_element_type=jnp.float32))
        mixed[:, lanes] = jnp.concatenate(results, axis=1).astype(jnp.bfloat16)

    @pl.loop(0, 6)
    def _(j):
        lanes = pl.ds(pl.multiple_of(j * 256, 256), 256)
        out_ref[:, lanes] = jnp.dot(
            mixed[...], w_out[:, lanes], preferred_element_type=jnp.float32
        ).astype(jnp.bfloat16)


def compute(slots, fine, up, x, w, fine_gain, coarse_gain):
    vmem = pl.BlockSpec(memory_space=pltpu.VMEM)
    return pl.pallas_call(
        compute_kernel,
        out_shape=jax.ShapeDtypeStruct(fine.shape, jnp.bfloat16),
        in_specs=[pl.BlockSpec(memory_space=pltpu.SMEM)] + [vmem] * 6,
        out_specs=vmem,
        scratch_shapes=[
            pltpu.VMEM((512, D), jnp.bfloat16),
            pltpu.VMEM((256, D), jnp.bfloat16),
            pltpu.VMEM((512, HD), jnp.bfloat16),
            pltpu.VMEM((256, D), jnp.bfloat16),
            pltpu.VMEM((512, HD), jnp.bfloat16),
            pltpu.VMEM((HD, D), jnp.bfloat16),
        ],
        compiler_params=pltpu.CompilerParams(vmem_limit_bytes=56 << 20),
    )(slots, fine, up, x, w, fine_gain, coarse_gain)


def body(coarse, fine_embed, fine_gain, coarse_gain, w_query, w_kv, w_out, readers, picks):
    tile = lax.axis_index("tile")
    z = tile // 2
    strips = jnp.arange(NT, dtype=jnp.int32)
    blk = jnp.sum(jnp.where(readers[:, :, None] == strips, picks[:, :, None], 0), axis=1)
    mine = lax.dynamic_index_in_dim(readers, tile, 0, keepdims=False)
    lane = mine % 2
    slots = lane * NZ + ((z - mine // 2) * (1 - 2 * lane)) % NZ

    def slabs(w):
        return w.reshape(48, -1, 128).transpose(1, 0, 2)

    out_pairs = w_out.reshape(24, 2, 6, 128).transpose(2, 1, 0, 3).reshape(6, 48, 128)
    shard = jnp.concatenate([slabs(w_query), slabs(w_kv), out_pairs], axis=0).reshape(4, 2, 3, 48, 128)
    w, x, up = gather(coarse.reshape(8, BLOCK, D), shard, blk)
    return compute(
        slots, fine_embed, up, x, w.reshape(24, NZ, 2, 48, 128), fine_gain.reshape(1, D), coarse_gain.reshape(1, D)
    )


def solution(mesh):
    placed = (
        P(("img", "tile"), None),
        P(("img", "tile"), None),
        P(),
        P(),
        P("tile", None),
        P("tile", None),
        P("tile", None),
        P("img", None),
        P("img", None),
    )
    return jax.shard_map(
        body, mesh=mesh, in_specs=placed, out_specs=P(("img", "tile"), None), check_vma=False
    )
```

time: 281 us -> 132 us (0.47)
  waiting for transfers between devices: 166 us -> 0 us
  Pallas kernels: 0 us -> 121 us
  starting transfers between devices: 61.2 us -> 0 us
  matrix products: 20.3 us -> 0 us
  between operations: 13.7 us -> 0.04 us
  other arithmetic: 7 us -> 1.53 us
    pallas_call x0 -> x2, Pallas kernels: none -> 121 us  [the longest x1 96.2 us: gather(): pl.pallas_call(gather_kernel, out_shape=(jax.ShapeDtypeStruct((4, 2, 3, N...]
    all_gather x3 -> x0, waiting for transfers between devices: 100 us -> none  [the longest x1 79.4 us: body(): lax.all_gather(w_kv, 'tile', axis=0, tiled=True)]
    ppermute x14 -> x0, waiting for transfers between devices: 64.7 us -> none  [passed_along(): lax.ppermute(value, axis, [(source, source + steps) for source in range(f...]
    ppermute x14 -> x0, starting transfers between devices: 52.9 us -> none  [passed_along(): lax.ppermute(value, axis, [(source, source + steps) for source in range(f...]
    dot_general x4 -> x0, matrix products: 15.6 us -> none  [the longest x3 12.1 us: add_rows(): return jnp.dot(left_rows, piece, preferred_element_type=jnp.float32)]
    all_to_all x1 -> x0, starting transfers between devices: 8.2 us -> none  [body(): lax.all_to_all(value_slots, 'tile', split_axis=0, concat_axis=0, tiled=True)]
    reshape x0 -> x5, local copies, waits for them, and re-layouts: none -> 5.6 us  [the longest x2 2.02 us: slabs(): return w.reshape(48, -1, 128).transpose(1, 0, 2)]
    convert_element_type x2 -> x0, local copies, waits for them, and re-layouts: 5.32 us -> none  [the longest x1 3.91 us: body(): hidden = fine_embed.astype(jnp.float32) + upsampled.astype(jnp.float32)]
  transfers between devices with their start and end apart: 18 -> 0, of which waited for: 9 -> 0; matrix products, arithmetic and copies ran while one was open for 12% -> 0% of each run, Pallas kernels for 0% -> 0%
where the time goes in v1:
time: 132 us; the launch traced here: 131 us
  Pallas kernels  121 us (92%)
  local copies, waits for them, and re-layouts  8.78 us (7%)
  other arithmetic  1.53 us (1%)
    pallas_call x1, Pallas kernels, gather(): pl.pallas_call(gather_kernel, out_shape=(jax.ShapeDtypeStruct((4, 2, 3, N...  96.2 us
    pallas_call x1, Pallas kernels, compute(): pl.pallas_call(compute_kernel, out_shape=jax.ShapeDtypeStruct(fine.shape,...  24.5 us

profile of v1, /device:TPU:1, one launch (start us, length us, event | category | flops | bytes accessed | tf_op | source)
XLA Modules:
  0.0 131.1 jit_solution(3905161330030698770)
XLA Ops:
  0.0 0.9 dynamic-slice_reduce_fusion
  0.9 0.6 fusion.slot_ref
  1.5 1.3 reshape.36.fine_gain_ref
  2.7 1.3 reshape.37.coarse_gain_ref
  4.0 0.8 copy.22
  4.8 0.8 copy.21
  5.6 0.8 select_reduce_fusion.blk_ref
  6.4 1.0 reshape.30
  7.4 1.0 reshape.32
  8.4 1.0 reshape.31
  9.4 0.1 pad_maximum_fusion
  9.6 0.8 copy.20
  10.3 96.2 %shard_map.91 = (bf16[4,2,3,16,2,48,128]{6,5,4,3,2,1,0:T(8,128)(2,1)}, bf16[2,16,16,1536]{3,2,1,0:T(8,128)(2,1)}, bf16[8,16,1536]{2,1,0:T(8,128)(2,1)}) custom-call(bf16[8,16,1536]{2,1,0:T(8,128)(2,1)} %bitcast.11, bf16[4,2,3,48,128]{4,3,2,1,0:T(8,128)(2,1)} %bitcast.8, s32[32,32]{1,0:T(8,128)} %select_reduce_fusion.blk_ref), custom_call_target="tpu_custom_call" | custom-call | tf_op jit(solution)/shard_map/pallas_call | solution.py:261
  106.6 24.5 %shard_map.92 = bf16[512,1536]{1,0:T(8,128)(2,1)} custom-call(s32[16]{0:T(128)} %fusion.slot_ref, bf16[512,1536]{1,0:T(8,128)(2,1)} %fine_ref.1, bf16[8,16,1536]{2,1,0:T(8,128)(2,1)} %get-tuple-element.8.up_ref, bf16[2,16,16,1536]{3,2,1,0:T(8,128)(2,1)} %get-tuple-element.9.x_ref, bf16[24,16,2,48,128]{4,3,2,1,0:T(8,128)(2,1)} %bitcast.7, ...), custom_call_target="tpu_custom_call" | custom-call | tf_op jit(solution)/shard_map/pallas_call | solution.py:368
  (1 shorter events, 0.0 us)

commit v2 on v0

v2 whole, which is shorter than its diff:
```python
import jax
import jax.numpy as jnp
from jax import lax
from jax.experimental import pallas as pl
from jax.experimental.pallas import tpu as pltpu
from jax.sharding import PartitionSpec as P

HEADS = 12
HDIM = 64
BLOCK = 16
NZ = 16
NT = 32
D = 1536
HD = 768
LONG = 5
SHORT = 4
EPSILON = 1e-06
LOG2E = 1.4426950408889634
MESH = pl.DeviceIdType.MESH


def wrap(value, size):
    return lax.rem(value + size, size)


def normalized(values, gain):
    inverse = lax.rsqrt(jnp.mean(values * values, axis=-1, keepdims=True) + EPSILON)
    return (values * inverse * gain).astype(jnp.bfloat16)


def kernel(
    coarse_ref, wq_ref, wkv_ref, wo_ref, blk_ref, readers_ref, fine_hbm, fine_gain_ref, coarse_gain_ref, out_hbm,
    w_ref, x_ref, up_ref, l1, l2, l3, l4, l5, s1, s2, s3, s4, stage, far_l, far_s,
    fine, fine_n, coarse_n, query, keyval, mixed, w_out, out, gains,
    local_sem, out_sem, zw_send, zw_recv, c_send, c_recv, far_send, far_recv, near_send, near_recv, up_send, up_recv,
    a_send, a_recv, b_send, b_recv, d_send, d_recv,
):
    img, tile = lax.axis_index("img"), lax.axis_index("tile")
    z, core = tile // 2, lax.rem(tile, 2)
    other = 1 - core
    sign = 1 - 2 * core
    gx, gy = img // 4, lax.rem(img, 4)
    a = jnp.where(core == 0, gx, gy)
    b = jnp.where(core == 0, gy, gx)
    bp = lax.rem(b, 2)

    fine_copy = pltpu.make_async_copy(fine_hbm, fine, local_sem)
    fine_copy.start()

    def along(steps):
        return wrap(z + sign * steps, NZ)

    def on_z(steps, which):
        return {"img": img, "tile": along(steps) * 2 + which}

    def on_plane(first, second):
        first, second = wrap(first, 4), wrap(second, 4)
        return {"img": jnp.where(core == 0, first * 4 + second, second * 4 + first), "tile": tile}

    sibling = {"img": img, "tile": z * 2 + other}
    a_up, a_down = on_plane(a + 1, b), on_plane(a - 1, b)
    b_up, b_down = on_plane(a, b + 1), on_plane(a, b - 1)
    ahead, behind = on_z(1, core), on_z(-1, core)

    partners = [sibling, a_up, a_down, b_up, b_down]
    partners += [on_z(j, which) for j in (-3, -2, -1, 1, 2, 3) for which in (core, other)]
    barrier = pltpu.get_barrier_semaphore()
    for partner in partners:
        pl.semaphore_signal(barrier, inc=1, device_id=partner, device_id_type=MESH)

    piece_index = 2 * a + bp

    @pl.when(piece_index < 2)
    def _():
        for i in range(3):
            lanes = pl.ds(pl.multiple_of((3 * piece_index + i) * 128, 128), 128)
            w_ref[a, bp, i, z, core] = wq_ref[:, lanes]

    @pl.when((piece_index >= 2) & (piece_index < 6))
    def _():
        for i in range(3):
            lanes = pl.ds(pl.multiple_of((3 * piece_index + i - 6) * 128, 128), 128)
            w_ref[a, bp, i, z, core] = wkv_ref[:, lanes]

    @pl.when(piece_index >= 6)
    def _():
        for i in range(3):
            slab = 3 * piece_index + i - 18
            upper = wo_ref[:, pl.ds(pl.multiple_of(slab * 128, 128), 128)].astype(jnp.float32)
            lower = wo_ref[:, pl.ds(pl.multiple_of((slab + 6) * 128, 128), 128)].astype(jnp.float32)
            w_ref[a, bp, i, z, core] = jnp.concatenate([upper, lower], axis=0).astype(jnp.bfloat16)

    pl.semaphore_wait(barrier, len(partners))

    def remote(src, dst, send, recv, device):
        return pltpu.make_async_remote_copy(
            src_ref=src, dst_ref=dst, send_sem=send, recv_sem=recv, device_id=device, device_id_type=MESH
        )

    pending = []

    def go(copy):
        copy.start()
        pending.append(copy)
        return copy

    def drain():
        for copy in pending:
            copy.wait_send()
        pending.clear()

    def place(m):
        return along(-m if m <= 8 else m - 8)

    def group(step):
        return [0] if step == 0 else [8] if step == 8 else [step, 8 + step]

    zw, x1, x2, y, d1, d2, cc = {}, {}, {}, {}, {}, {}, {}

    def zw_start(step):
        for m in group(step):
            where = w_ref.at[a, bp, :, along(1 - m if m <= 8 else m - 9), core]
            zw[m] = go(remote(where, where, zw_send.at[m], zw_recv.at[m], ahead if m <= 8 else behind))

    def x1_start(step):
        for m in group(step):
            where = w_ref.at[a, bp, :, place(m), core]
            for k, device in enumerate((a_up, a_down)):
                slot = 2 * m + k
                x1[m, k] = go(remote(where, where, a_send.at[slot], a_recv.at[slot], device))

    def x2_start(step):
        for m in group(step):
            rising = m < 8
            where = w_ref.at[wrap(a - 1 if rising else a + 1, 4), bp, :, place(m), core]
            x2[m] = go(remote(where, where, a_send.at[32 + m], a_recv.at[32 + m], a_up if rising else a_down))

    def y_start(step):
        for m in group(step):
            where = w_ref.at[:, bp, :, place(m), core]
            y[m] = go(remote(where, where, b_send.at[m], b_recv.at[m], b_up if m < 8 else b_down))
            d1[m] = go(remote(where, where, d_send.at[m], d_recv.at[m], sibling))

    def d2_start(step):
        for m in group(step):
            where = w_ref.at[:, 1 - bp, :, place(m), core]
            d2[m] = go(remote(where, where, d_send.at[16 + m], d_recv.at[16 + m], sibling))

    long_buf = [coarse_ref, l1, l2, l3, l4, l5]
    short_buf = [coarse_ref, s1, s2, s3, s4]

    def c_copy(step, half, forward):
        bufs = long_buf if forward else short_buf
        slot = 2 * (step - 1 if forward else LONG + step - 1) + half
        part = pl.ds(4 * half, 4)
        return remote(
            bufs[step - 1].at[part], bufs[step].at[part], c_send.at[slot], c_recv.at[slot],
            ahead if forward else behind,
        )

    def c_start(step, half):
        if step <= LONG:
            cc[step, half, True] = go(c_copy(step, half, True))
        if step <= SHORT:
            cc[step, half, False] = go(c_copy(step, half, False))

    def c_pass(step, half):
        if step <= LONG:
            cc[step, half, True].wait_recv()
        if step <= SHORT:
            cc[step, half, False].wait_recv()
        if step < LONG:
            c_start(step + 1, half)

    conditional = []

    def share(buf, steps, index, distance):
        strip = along(steps) * 2 + core
        x_ref[core, distance] = buf[blk_ref[tile, strip]]
        stage[index] = buf[blk_ref[z * 2 + other, strip]]
        go(remote(stage.at[index], x_ref.at[core, distance], near_send.at[index], near_recv.at[index], sibling))
        if abs(steps) <= 3:
            position = lax.rem(z, 4) + sign * steps
            inside = (position >= 0) & (position < 4)
            column = lax.rem(tile, 8)
            column_other = lax.rem(z * 2 + other, 8)
            kept = jnp.clip(position, 0, 3)
            row = 2 * kept + core
            sent = remote(
                buf.at[column_other], up_ref.at[row], up_send.at[index], up_recv.at[kept], sibling
            )

            @pl.when(inside)
            def _():
                up_ref[row] = buf[column]
                sent.start()

            conditional.append((inside, sent))

    def share_step(step):
        if step == 0:
            share(coarse_ref, 0, 0, 0)
            return
        if step <= LONG:
            share(long_buf[step], -step, step, step)
        if step <= SHORT:
            share(short_buf[step], step, LONG + step, NZ - step)

    far = []

    def send_far(forward):
        buf = l5 if forward else s4
        held = LONG if forward else SHORT
        picked = far_l if forward else far_s
        strip = along(-LONG if forward else SHORT) * 2 + core
        for j in (3, 2, 1):
            target = along(j if forward else -j)
            distance = held + j if forward else NZ - held - j
            for e in range(2):
                which = core if e == 0 else other
                slot = (0 if forward else 6) + 2 * (j - 1) + e
                picked[2 * (j - 1) + e] = buf[blk_ref[target * 2 + which, strip]]
                far.append(go(remote(
                    picked.at[2 * (j - 1) + e], x_ref.at[core, distance], far_send.at[slot], far_recv.at[slot],
                    {"img": img, "tile": target * 2 + which},
                )))

    def tick(i):
        if i <= 8:
            if i > 0:
                for m in group(i):
                    zw[m].wait_recv()
            if i < 8:
                zw_start(i + 1)
            x1_start(i)
        if 1 <= i <= 9:
            for m in group(i - 1):
                x1[m, 0].wait_recv()
                x1[m, 1].wait_recv()
            x2_start(i - 1)
        if 2 <= i <= 10:
            for m in group(i - 2):
                x2[m].wait_recv()
            y_start(i - 2)
        if i >= 3:
            for m in group(i - 3):
                y[m].wait_recv()
            d2_start(i - 3)

    c_start(1, 0)
    tick(0)
    c_start(1, 1)
    share_step(0)
    tick(1)
    c_pass(1, 0)
    tick(2)
    tick(3)
    c_pass(1, 1)
    tick(4)
    c_pass(2, 0)
    share_step(1)
    tick(5)
    tick(6)
    c_pass(2, 1)
    tick(7)
    c_pass(3, 0)
    share_step(2)
    tick(8)
    tick(9)
    c_pass(3, 1)
    tick(10)
    tick(11)
    share_step(3)
    c_pass(4, 0)

    for index, gain_ref in enumerate((fine_gain_ref, coarse_gain_ref)):
        gains[index] = gain_ref[...].reshape(1, D)
    fine_copy.wait()
    for row in range(4):
        remote(coarse_ref.at[0], up_ref.at[row], up_send.at[row], up_recv.at[row], sibling).wait_recv()

    rows = lax.broadcasted_iota(jnp.int32, (32, BLOCK), 0) // 2
    spread = (rows == lax.broadcasted_iota(jnp.int32, (32, BLOCK), 1)).astype(jnp.bfloat16)

    def fine_norm(first, last):
        @pl.loop(first, last)
        def _(i):
            up = jnp.dot(spread, up_ref[i], preferred_element_type=jnp.float32)
            for half in range(2):
                part = pl.ds(pl.multiple_of(i * 64 + half * 32, 32), 32)
                hidden = fine[part, :].astype(jnp.float32) + up
                fine_n[part, :] = normalized(hidden, gains[0])

    def slab(index):
        return w_ref[index // 6, lax.rem(index // 3, 2), lax.rem(index, 3)].reshape(D, 128)

    def project_query():
        @pl.loop(0, 3)
        def _(j):
            pair = jnp.concatenate([slab(2 * j), slab(2 * j + 1)], axis=1)
            query[:, pl.ds(pl.multiple_of(j * 256, 256), 256)] = jnp.dot(
                fine_n[...], pair, preferred_element_type=jnp.float32
            ).astype(jnp.bfloat16)

    def order_out():
        @pl.loop(0, NZ)
        def _(k):
            part = pl.ds(pl.multiple_of(k * 48, 48), 48)
            for j in range(6):
                even = w_ref[3, j // 3, j % 3, k, 0].astype(jnp.float32)
                odd = w_ref[3, j // 3, j % 3, k, 1].astype(jnp.float32)
                for half in range(2):
                    cut = slice(24 * half, 24 * half + 24)
                    w_out[part, pl.ds((j + 6 * half) * 128, 128)] = jnp.concatenate(
                        [even[cut], odd[cut]], axis=0
                    ).astype(jnp.bfloat16)

    fine_norm(0, 8)
    c_pass(4, 1)
    send_far(False)
    share_step(4)
    c_pass(5, 0)
    for m in range(16):
        d1[m].wait_recv()
        d2[m].wait_recv()
    project_query()
    c_pass(5, 1)
    send_far(True)
    share_step(5)
    order_out()
    drain()
    for inside, copy in conditional:
        pl.when(inside)(copy.wait_send)
    for index in range(LONG + SHORT + 1):
        remote(stage.at[index], x_ref.at[core, index], near_send.at[index], near_recv.at[index], sibling).wait_recv()
    for copy in far:
        copy.wait_recv()

    @pl.loop(0, 16)
    def _(r):
        reader = readers_ref[r, tile]
        lane = lax.rem(reader, 2)
        distance = lax.rem((z - reader // 2) * (1 - 2 * lane) + NZ, NZ)
        values = x_ref[lane, distance].astype(jnp.float32)
        coarse_n[pl.ds(pl.multiple_of(r * BLOCK, BLOCK), BLOCK), :] = normalized(values, gains[1])

    def projected(p):
        pair = jnp.concatenate([slab(6 + p), slab(12 + p)], axis=1)
        return jnp.dot(coarse_n[...], pair, preferred_element_type=jnp.float32).astype(jnp.bfloat16)

    low = lax.broadcasted_iota(jnp.int32, (1, 128), 1) < HDIM
    keyval[0] = projected(0)

    @pl.loop(0, HEADS // 2, unroll=2)
    def _(p):
        lanes = pl.ds(pl.multiple_of(p * 128, 128), 128)
        both = keyval[lax.rem(p, 2)]
        keyval[lax.rem(p + 1, 2)] = projected(jnp.minimum(p + 1, HEADS // 2 - 1))
        keys, values = both[:, :128], both[:, 128:]
        zero, one = jnp.zeros_like(keys), jnp.ones_like(values)
        key_pair = [jnp.where(low, keys, zero), jnp.where(low, zero, keys)]
        value_pair = [jnp.where(low, values, one), jnp.where(low, one, values)]
        queries = query[:, lanes]
        results = []
        for h in range(2):
            scores = lax.dot_general(
                queries, key_pair[h], (((1,), (1,)), ((), ())), preferred_element_type=jnp.float32
            )
            top = jnp.max(scores, axis=-1, keepdims=True)
            exponent = jnp.exp2((scores - top) * (HDIM ** (-0.5) * LOG2E)).astype(jnp.bfloat16)
            results.append(jnp.dot(exponent, value_pair[h], preferred_element_type=jnp.float32))
        total = pltpu.roll(jnp.where(low, results[1], results[0]), HDIM, 1)
        mixed[:, lanes] = (jnp.where(low, results[0], results[1]) / total).astype(jnp.bfloat16)

    for j in range(3):
        lanes = pl.ds(j * 512, 512)
        out[j] = jnp.dot(mixed[...], w_out[:, lanes], preferred_element_type=jnp.float32).astype(jnp.bfloat16)
        pltpu.make_async_copy(out.at[j], out_hbm.at[:, lanes], out_sem.at[j]).start()
    for j in range(3):
        pltpu.make_async_copy(out.at[j], out_hbm.at[:, pl.ds(j * 512, 512)], out_sem.at[j]).wait()


def body(coarse, fine_embed, fine_gain, coarse_gain, w_query, w_kv, w_out, readers, picks):
    strips = jnp.arange(NT, dtype=jnp.int32)
    readers, picks = readers.T, picks.T
    blk = jnp.sum(jnp.where(readers[:, :, None] == strips, picks[:, :, None], 0), axis=0)
    vmem, smem = pl.BlockSpec(memory_space=pltpu.VMEM), pl.BlockSpec(memory_space=pltpu.SMEM)
    hbm = pl.BlockSpec(memory_space=pl.ANY)
    bf16 = jnp.bfloat16
    strip = pltpu.VMEM((8, BLOCK, D), bf16)
    near = LONG + SHORT + 1

    def dma(count):
        return pltpu.SemaphoreType.DMA((count,))

    return pl.pallas_call(
        kernel,
        out_shape=jax.ShapeDtypeStruct(fine_embed.shape, bf16),
        in_specs=[vmem] * 4 + [smem] * 2 + [hbm, vmem, vmem],
        out_specs=hbm,
        scratch_shapes=[
            pltpu.VMEM((4, 2, 3, NZ, 2, 48, 128), bf16),
            pltpu.VMEM((2, NZ, BLOCK, D), bf16),
            strip,
        ] + [strip] * (LONG + SHORT) + [
            pltpu.VMEM((near, BLOCK, D), bf16),
            pltpu.VMEM((6, BLOCK, D), bf16),
            pltpu.VMEM((6, BLOCK, D), bf16),
            pltpu.VMEM((512, D), bf16),
            pltpu.VMEM((512, D), bf16),
            pltpu.VMEM((256, D), bf16),
            pltpu.VMEM((512, HD), bf16),
            pltpu.VMEM((2, 256, 256), bf16),
            pltpu.VMEM((512, HD), bf16),
            pltpu.VMEM((HD, D), bf16),
            pltpu.VMEM((3, 512, 512), bf16),
            pltpu.VMEM((2, 1, D), jnp.float32),
            pltpu.SemaphoreType.DMA, dma(3),
            dma(16), dma(16),
            dma(2 * (LONG + SHORT)), dma(2 * (LONG + SHORT)),
            dma(12), dma(12),
            dma(near), dma(near),
            dma(near), dma(4),
            dma(48), dma(48),
            dma(16), dma(16),
            dma(32), dma(32),
        ],
        compiler_params=pltpu.CompilerParams(
            collective_id=0, has_side_effects=True, vmem_limit_bytes=56 << 20
        ),
    )(coarse.reshape(8, BLOCK, D), w_query, w_kv, w_out, blk, readers, fine_embed, fine_gain, coarse_gain)


def solution(mesh):
    placed = (
        P(("img", "tile"), None),
        P(("img", "tile"), None),
        P(),
        P(),
        P("tile", None),
        P("tile", None),
        P("tile", None),
        P("img", None),
        P("img", None),
    )
    return jax.shard_map(
        body, mesh=mesh, in_specs=placed, out_specs=P(("img", "tile"), None), check_vma=False
    )
```

time: 281 us -> 101 us (0.36)
  waiting for transfers between devices: 166 us -> 0 us
  Pallas kernels: 0 us -> 96.2 us
  starting transfers between devices: 61.2 us -> 0 us
  matrix products: 20.3 us -> 0 us
  between operations: 13.7 us -> 0.01 us
  local copies, waits for them, and re-layouts: 11.5 us -> 2.65 us
  other arithmetic: 7 us -> 1.53 us
    all_gather x3 -> x0, waiting for transfers between devices: 100 us -> none  [the longest x1 79.4 us: body(): lax.all_gather(w_kv, 'tile', axis=0, tiled=True)]
    pallas_call x0 -> x1, Pallas kernels: none -> 96.2 us  [body(): pl.pallas_call(kernel, out_shape=jax.ShapeDtypeStruct(fine_embed.shape, b...]
    ppermute x14 -> x0, waiting for transfers between devices: 64.7 us -> none  [passed_along(): lax.ppermute(value, axis, [(source, source + steps) for source in range(f...]
    ppermute x14 -> x0, starting transfers between devices: 52.9 us -> none  [passed_along(): lax.ppermute(value, axis, [(source, source + steps) for source in range(f...]
    dot_general x4 -> x0, matrix products: 15.6 us -> none  [the longest x3 12.1 us: add_rows(): return jnp.dot(left_rows, piece, preferred_element_type=jnp.float32)]
    all_to_all x1 -> x0, starting transfers between devices: 8.2 us -> none  [body(): lax.all_to_all(value_slots, 'tile', split_axis=0, concat_axis=0, tiled=True)]
    convert_element_type x2 -> x0, local copies, waits for them, and re-layouts: 5.32 us -> none  [the longest x1 3.91 us: body(): hidden = fine_embed.astype(jnp.float32) + upsampled.astype(jnp.float32)]
    sub x1 -> x0, matrix products: 4.78 us -> none  [attend(): exponent = jnp.exp(scores - maximum)]
  transfers between devices with their start and end apart: 18 -> 0, of which waited for: 9 -> 0; matrix products, arithmetic and copies ran while one was open for 12% -> 0% of each run, Pallas kernels for 0% -> 0%
where the time goes in v2:
time: 101 us; the launch traced here: 100 us
  Pallas kernels  96.2 us (95%)
  local copies, waits for them, and re-layouts  2.65 us (3%)
  other arithmetic  1.53 us (2%)
    pallas_call x1, Pallas kernels, body(): pl.pallas_call(kernel, out_shape=jax.ShapeDtypeStruct(fine_embed.shape, b...  96.2 us
    unnamed x1, local copies, waits for them, and re-layouts  2.65 us

profile of v2, /device:TPU:1, one launch (start us, length us, event | category | flops | bytes accessed | tf_op | source)
XLA Modules:
  0.0 100.4 jit_solution(15817259443194035707)
XLA Ops:
  0.0 1.5 %select_reduce_fusion.blk_ref = s32[32,32]{1,0:T(8,128)} fusion(s32[16,32]{1,0:T(8,128)} %bitcast.6, s32[16,32]{1,0:T(8,128)} %bitcast.4), kind=kLoop, calls=%fused_computation | loop fusion | flops 48128 | bytes 8192 | tf_op jit(solution)/shard_map/reduce_sum | solution.py:386
  1.5 96.2 %shard_map.91 = bf16[512,1536]{1,0:T(8,128)(2,1)} custom-call(bf16[8,16,1536]{2,1,0:T(8,128)(2,1)} %bitcast.3, bf16[48,768]{1,0:T(8,128)(2,1)} %wq_ref.1, bf16[48,1536]{1,0:T(8,128)(2,1)} %wkv_ref.1, bf16[24,1536]{1,0:T(8,128)(2,1)} %wo_ref.1, s32[32,32]{1,0:T(8,128)} %select_reduce_fusion.blk_ref, s32[16,32]{1,0:T(8,128)} %bitcast.5, ...), custom_call_target="tpu_custom_call" | custom-call | tf_op jit(solution)/shard_map/pallas_call | solution.py:396
  97.8 2.7 %copy.11 = bf16[512,1536]{1,0:T(8,128)(2,1)} copy(bf16[512,1536]{1,0:T(8,128)(2,1)} %shard_map.91) | data formatting | bytes 3145728

commit v3 on v2

--- a/solution.py
+++ b/solution.py
@@ -29,11 +29,11 @@
 
 
 def kernel(
-    coarse_ref, wq_ref, wkv_ref, wo_ref, blk_ref, readers_ref, fine_hbm, fine_gain_ref, coarse_gain_ref, out_hbm,
+    coarse_ref, wq_ref, wkv_ref, wo_ref, readers_ref, reader_rows, pick_rows, fine_hbm, fine_gain_ref, coarse_gain_ref, mixed_hbm, w_out_hbm,
     w_ref, x_ref, up_ref, l1, l2, l3, l4, l5, s1, s2, s3, s4, stage, far_l, far_s,
-    fine, fine_n, coarse_n, query, keyval, mixed, w_out, out, gains,
-    local_sem, out_sem, zw_send, zw_recv, c_send, c_recv, far_send, far_recv, near_send, near_recv, up_send, up_recv,
-    a_send, a_recv, b_send, b_recv, d_send, d_recv,
+    fine, fine_n, coarse_n, query, keyval, mixed, w_out, gains, blk_rows, blk,
+    local_sem, blk_sem, out_sem, zw_send, zw_recv, c_send, c_recv, far_send, far_recv, near_send, near_recv, up_send, up_recv,
+    a_send, a_recv, a2_send, a2_recv, b_send, b_recv, d_send, d_recv,
 ):
     img, tile = lax.axis_index("img"), lax.axis_index("tile")
     z, core = tile // 2, lax.rem(tile, 2)
@@ -68,6 +68,13 @@
     for partner in partners:
         pl.semaphore_signal(barrier, inc=1, device_id=partner, device_id_type=MESH)
 
+    for strip in range(NT):
+        blk_rows[strip : strip + 1, :] = jnp.sum(
+            jnp.where(reader_rows[...] == strip, pick_rows[...], 0), axis=0, keepdims=True
+        )
+    blk_copy = pltpu.make_async_copy(blk_rows, blk, blk_sem)
+    blk_copy.start()
+
     piece_index = 2 * a + bp
 
     @pl.when(piece_index < 2)
@@ -97,17 +104,19 @@
             src_ref=src, dst_ref=dst, send_sem=send, recv_sem=recv, device_id=device, device_id_type=MESH
         )
 
-    pending = []
-
     def go(copy):
         copy.start()
-        pending.append(copy)
-        return copy
 
     def drain():
-        for copy in pending:
-            copy.wait_send()
-        pending.clear()
+        whole(shards(15), zw_send, zw_recv.at[0]).wait_send()
+        whole(w_ref.at[a, bp], a_send, a_recv.at[0]).wait_send()
+        whole(shards(16), a2_send, a2_recv.at[0]).wait_send()
+        whole(w_ref.at[:, bp, :, :, core], b_send, b_recv.at[0]).wait_send()
+        whole(w_ref.at[:, :, :, :, core], d_send, d_recv).wait_send()
+        whole(w_ref.at[pl.ds(0, 3), :, :, :, core], c_send, c_recv.at[0]).wait_send()
+        whole(x_ref.at[0, pl.ds(0, LONG + SHORT + 1)], near_send, near_recv).wait_send()
+        whole(x_ref.at[0, pl.ds(0, 12)], far_send, far_recv).wait_send()
+        whole(up_ref.at[pl.ds(0, 4)], up_send, up_recv).wait_send()
 
     def place(m):
         return along(-m if m <= 8 else m - 8)
@@ -115,70 +124,70 @@
     def group(step):
         return [0] if step == 0 else [8] if step == 8 else [step, 8 + step]
 
-    zw, x1, x2, y, d1, d2, cc = {}, {}, {}, {}, {}, {}, {}
+    def whole(ref, send, recv):
+        return remote(ref, ref, send, recv, sibling)
+
+    def shards(count):
+        return w_ref.at[a, bp, :, pl.ds(0, count), core]
+
 
     def zw_start(step):
         for m in group(step):
             where = w_ref.at[a, bp, :, along(1 - m if m <= 8 else m - 9), core]
-            zw[m] = go(remote(where, where, zw_send.at[m], zw_recv.at[m], ahead if m <= 8 else behind))
+            go(remote(where, where, zw_send, zw_recv.at[step - 1], ahead if m <= 8 else behind))
 
     def x1_start(step):
         for m in group(step):
             where = w_ref.at[a, bp, :, place(m), core]
-            for k, device in enumerate((a_up, a_down)):
-                slot = 2 * m + k
-                x1[m, k] = go(remote(where, where, a_send.at[slot], a_recv.at[slot], device))
+            for device in (a_up, a_down):
+                go(remote(where, where, a_send, a_recv.at[step], device))
 
     def x2_start(step):
         for m in group(step):
             rising = m < 8
             where = w_ref.at[wrap(a - 1 if rising else a + 1, 4), bp, :, place(m), core]
-            x2[m] = go(remote(where, where, a_send.at[32 + m], a_recv.at[32 + m], a_up if rising else a_down))
+            go(remote(where, where, a2_send, a2_recv.at[step], a_up if rising else a_down))
 
     def y_start(step):
         for m in group(step):
             where = w_ref.at[:, bp, :, place(m), core]
-            y[m] = go(remote(where, where, b_send.at[m], b_recv.at[m], b_up if m < 8 else b_down))
-            d1[m] = go(remote(where, where, d_send.at[m], d_recv.at[m], sibling))
+            go(remote(where, where, b_send, b_recv.at[step], b_up if m < 8 else b_down))
+            go(remote(where, where, d_send, d_recv, sibling))
 
     def d2_start(step):
         for m in group(step):
             where = w_ref.at[:, 1 - bp, :, place(m), core]
-            d2[m] = go(remote(where, where, d_send.at[16 + m], d_recv.at[16 + m], sibling))
+            go(remote(where, where, d_send, d_recv, sibling))
 
     long_buf = [coarse_ref, l1, l2, l3, l4, l5]
     short_buf = [coarse_ref, s1, s2, s3, s4]
 
     def c_copy(step, half, forward):
         bufs = long_buf if forward else short_buf
-        slot = 2 * (step - 1 if forward else LONG + step - 1) + half
+        slot = 2 * (step - 1) + half
         part = pl.ds(4 * half, 4)
         return remote(
-            bufs[step - 1].at[part], bufs[step].at[part], c_send.at[slot], c_recv.at[slot],
+            bufs[step - 1].at[part], bufs[step].at[part], c_send, c_recv.at[slot],
             ahead if forward else behind,
         )
 
     def c_start(step, half):
         if step <= LONG:
-            cc[step, half, True] = go(c_copy(step, half, True))
+            c_copy(step, half, True).start()
         if step <= SHORT:
-            cc[step, half, False] = go(c_copy(step, half, False))
+            c_copy(step, half, False).start()
 
     def c_pass(step, half):
-        if step <= LONG:
-            cc[step, half, True].wait_recv()
-        if step <= SHORT:
-            cc[step, half, False].wait_recv()
+        blocks = 8 if step <= SHORT else 4
+        whole(x_ref.at[0, pl.ds(0, blocks)], c_send, c_recv.at[2 * (step - 1) + half]).wait_recv()
         if step < LONG:
             c_start(step + 1, half)
 
-    conditional = []
-
     def share(buf, steps, index, distance):
         strip = along(steps) * 2 + core
-        x_ref[core, distance] = buf[blk_ref[tile, strip]]
-        stage[index] = buf[blk_ref[z * 2 + other, strip]]
-        go(remote(stage.at[index], x_ref.at[core, distance], near_send.at[index], near_recv.at[index], sibling))
+        x_ref[core, distance] = buf[blk[strip, tile]]
+        stage[index] = buf[blk[strip, z * 2 + other]]
+        go(remote(stage.at[index], x_ref.at[core, distance], near_send, near_recv, sibling))
         if abs(steps) <= 3:
             position = lax.rem(z, 4) + sign * steps
             inside = (position >= 0) & (position < 4)
@@ -187,7 +196,7 @@
             kept = jnp.clip(position, 0, 3)
             row = 2 * kept + core
             sent = remote(
-                buf.at[column_other], up_ref.at[row], up_send.at[index], up_recv.at[kept], sibling
+                buf.at[column_other], up_ref.at[row], up_send, up_recv, sibling
             )
 
             @pl.when(inside)
@@ -195,7 +204,6 @@
                 up_ref[row] = buf[column]
                 sent.start()
 
-            conditional.append((inside, sent))
 
     def share_step(step):
         if step == 0:
@@ -205,8 +213,6 @@
             share(long_buf[step], -step, step, step)
         if step <= SHORT:
             share(short_buf[step], step, LONG + step, NZ - step)
-
-    far = []
 
     def send_far(forward):
         buf = l5 if forward else s4
@@ -218,66 +224,58 @@
             distance = held + j if forward else NZ - held - j
             for e in range(2):
                 which = core if e == 0 else other
-                slot = (0 if forward else 6) + 2 * (j - 1) + e
-                picked[2 * (j - 1) + e] = buf[blk_ref[target * 2 + which, strip]]
-                far.append(go(remote(
-                    picked.at[2 * (j - 1) + e], x_ref.at[core, distance], far_send.at[slot], far_recv.at[slot],
+                picked[2 * (j - 1) + e] = buf[blk[strip, target * 2 + which]]
+                go(remote(
+                    picked.at[2 * (j - 1) + e], x_ref.at[core, distance], far_send, far_recv,
                     {"img": img, "tile": target * 2 + which},
-                )))
+                ))
 
     def tick(i):
         if i <= 8:
             if i > 0:
-                for m in group(i):
-                    zw[m].wait_recv()
+                whole(shards(len(group(i))), zw_send, zw_recv.at[i - 1]).wait_recv()
             if i < 8:
                 zw_start(i + 1)
             x1_start(i)
         if 1 <= i <= 9:
-            for m in group(i - 1):
-                x1[m, 0].wait_recv()
-                x1[m, 1].wait_recv()
+            whole(shards(2 * len(group(i - 1))), a_send, a_recv.at[i - 1]).wait_recv()
             x2_start(i - 1)
         if 2 <= i <= 10:
-            for m in group(i - 2):
-                x2[m].wait_recv()
+            whole(shards(len(group(i - 2))), a2_send, a2_recv.at[i - 2]).wait_recv()
             y_start(i - 2)
-        if i >= 3:
-            for m in group(i - 3):
-                y[m].wait_recv()
-            d2_start(i - 3)
+        if 4 <= i <= 4 + 8:
+            count = len(group(i - 4))
+            whole(w_ref.at[:, bp, :, pl.ds(0, count), core], b_send, b_recv.at[i - 4]).wait_recv()
+            d2_start(i - 4)
 
     c_start(1, 0)
     tick(0)
     c_start(1, 1)
-    share_step(0)
+    blk_copy.wait()
     tick(1)
     c_pass(1, 0)
+    share_step(0)
     tick(2)
+    c_pass(1, 1)
+    share_step(1)
     tick(3)
-    c_pass(1, 1)
+    c_pass(2, 0)
     tick(4)
-    c_pass(2, 0)
-    share_step(1)
+    c_pass(2, 1)
+    share_step(2)
     tick(5)
+    c_pass(3, 0)
     tick(6)
-    c_pass(2, 1)
+    c_pass(3, 1)
+    share_step(3)
     tick(7)
-    c_pass(3, 0)
-    share_step(2)
+    c_pass(4, 0)
     tick(8)
-    tick(9)
-    c_pass(3, 1)
-    tick(10)
-    tick(11)
-    share_step(3)
-    c_pass(4, 0)
 
     for index, gain_ref in enumerate((fine_gain_ref, coarse_gain_ref)):
         gains[index] = gain_ref[...].reshape(1, D)
     fine_copy.wait()
-    for row in range(4):
-        remote(coarse_ref.at[0], up_ref.at[row], up_send.at[row], up_recv.at[row], sibling).wait_recv()
+    whole(up_ref.at[pl.ds(0, 4)], up_send, up_recv).wait_recv()
 
     rows = lax.broadcasted_iota(jnp.int32, (32, BLOCK), 0) // 2
     spread = (rows == lax.broadcasted_iota(jnp.int32, (32, BLOCK), 1)).astype(jnp.bfloat16)
@@ -315,28 +313,29 @@
                         [even[cut], odd[cut]], axis=0
                     ).astype(jnp.bfloat16)
 
-    fine_norm(0, 8)
     c_pass(4, 1)
     send_far(False)
     share_step(4)
+    tick(9)
+    fine_norm(0, 4)
+    tick(10)
+    fine_norm(4, 8)
+    tick(11)
     c_pass(5, 0)
-    for m in range(16):
-        d1[m].wait_recv()
-        d2[m].wait_recv()
-    project_query()
     c_pass(5, 1)
     send_far(True)
     share_step(5)
+    tick(12)
+    whole(w_ref.at[:, :, :, :, core], d_send, d_recv).wait_recv()
+    project_query()
     order_out()
+    w_out_copy = pltpu.make_async_copy(w_out, w_out_hbm, out_sem.at[HEADS // 2])
+    w_out_copy.start()
     drain()
-    for inside, copy in conditional:
-        pl.when(inside)(copy.wait_send)
-    for index in range(LONG + SHORT + 1):
-        remote(stage.at[index], x_ref.at[core, index], near_send.at[index], near_recv.at[index], sibling).wait_recv()
-    for copy in far:
-        copy.wait_recv()
-
-    @pl.loop(0, 16)
+    whole(x_ref.at[0, pl.ds(0, LONG + SHORT + 1)], near_send, near_recv).wait_recv()
+    whole(x_ref.at[0, pl.ds(0, 12)], far_send, far_recv).wait_recv()
+
+    @pl.loop(0, 16, unroll=4)
     def _(r):
         reader = readers_ref[r, tile]
         lane = lax.rem(reader, 2)
@@ -347,6 +346,10 @@
     def projected(p):
         pair = jnp.concatenate([slab(6 + p), slab(12 + p)], axis=1)
         return jnp.dot(coarse_n[...], pair, preferred_element_type=jnp.float32).astype(jnp.bfloat16)
+
+    def mixed_copy(p):
+        lanes = pl.ds(pl.multiple_of(p * 128, 128), 128)
+        return pltpu.make_async_copy(mixed.at[p], mixed_hbm.at[:, lanes], out_sem.at[p])
 
     low = lax.broadcasted_iota(jnp.int32, (1, 128), 1) < HDIM
     keyval[0] = projected(0)
@@ -370,34 +373,33 @@
             exponent = jnp.exp2((scores - top) * (HDIM ** (-0.5) * LOG2E)).astype(jnp.bfloat16)
             results.append(jnp.dot(exponent, value_pair[h], preferred_element_type=jnp.float32))
         total = pltpu.roll(jnp.where(low, results[1], results[0]), HDIM, 1)
-        mixed[:, lanes] = (jnp.where(low, results[0], results[1]) / total).astype(jnp.bfloat16)
-
-    for j in range(3):
-        lanes = pl.ds(j * 512, 512)
-        out[j] = jnp.dot(mixed[...], w_out[:, lanes], preferred_element_type=jnp.float32).astype(jnp.bfloat16)
-        pltpu.make_async_copy(out.at[j], out_hbm.at[:, lanes], out_sem.at[j]).start()
-    for j in range(3):
-        pltpu.make_async_copy(out.at[j], out_hbm.at[:, pl.ds(j * 512, 512)], out_sem.at[j]).wait()
+        mixed[p] = (jnp.where(low, results[0], results[1]) / total).astype(jnp.bfloat16)
+        mixed_copy(p).start()
+
+    for p in range(HEADS // 2):
+        mixed_copy(p).wait()
+    w_out_copy.wait()
 
 
 def body(coarse, fine_embed, fine_gain, coarse_gain, w_query, w_kv, w_out, readers, picks):
-    strips = jnp.arange(NT, dtype=jnp.int32)
-    readers, picks = readers.T, picks.T
-    blk = jnp.sum(jnp.where(readers[:, :, None] == strips, picks[:, :, None], 0), axis=0)
     vmem, smem = pl.BlockSpec(memory_space=pltpu.VMEM), pl.BlockSpec(memory_space=pltpu.SMEM)
     hbm = pl.BlockSpec(memory_space=pl.ANY)
     bf16 = jnp.bfloat16
     strip = pltpu.VMEM((8, BLOCK, D), bf16)
     near = LONG + SHORT + 1
 
-    def dma(count):
-        return pltpu.SemaphoreType.DMA((count,))
-
-    return pl.pallas_call(
+    dma = pltpu.SemaphoreType.DMA
+
+    def many(count):
+        return dma((count,))
+
+    mixed, w_out_whole = pl.pallas_call(
         kernel,
-        out_shape=jax.ShapeDtypeStruct(fine_embed.shape, bf16),
-        in_specs=[vmem] * 4 + [smem] * 2 + [hbm, vmem, vmem],
-        out_specs=hbm,
+        out_shape=(
+            jax.ShapeDtypeStruct((fine_embed.shape[0], HD), bf16), jax.ShapeDtypeStruct((HD, D), bf16)
+        ),
+        in_specs=[vmem] * 4 + [smem, vmem, vmem] + [hbm, vmem, vmem],
+        out_specs=(hbm, hbm),
         scratch_shapes=[
             pltpu.VMEM((4, 2, 3, NZ, 2, 48, 128), bf16),
             pltpu.VMEM((2, NZ, BLOCK, D), bf16),
@@ -411,24 +413,27 @@
             pltpu.VMEM((256, D), bf16),
             pltpu.VMEM((512, HD), bf16),
             pltpu.VMEM((2, 256, 256), bf16),
-            pltpu.VMEM((512, HD), bf16),
+            pltpu.VMEM((HEADS // 2, 512, 128), bf16),
             pltpu.VMEM((HD, D), bf16),
-            pltpu.VMEM((3, 512, 512), bf16),
             pltpu.VMEM((2, 1, D), jnp.float32),
-            pltpu.SemaphoreType.DMA, dma(3),
-            dma(16), dma(16),
-            dma(2 * (LONG + SHORT)), dma(2 * (LONG + SHORT)),
-            dma(12), dma(12),
-            dma(near), dma(near),
-            dma(near), dma(4),
-            dma(48), dma(48),
-            dma(16), dma(16),
-            dma(32), dma(32),
+            pltpu.VMEM((NT, NT), jnp.int32),
+            pltpu.SMEM((NT, NT), jnp.int32),
+            dma, dma, many(HEADS // 2 + 1),
+            dma, many(8),
+            dma, many(2 * LONG),
+            dma, dma,
+            dma, dma,
+            dma, dma,
+            dma, many(9),
+            dma, many(9),
+            dma, many(9),
+            dma, dma,
         ],
         compiler_params=pltpu.CompilerParams(
             collective_id=0, has_side_effects=True, vmem_limit_bytes=56 << 20
         ),
-    )(coarse.reshape(8, BLOCK, D), w_query, w_kv, w_out, blk, readers, fine_embed, fine_gain, coarse_gain)
+    )(coarse.reshape(8, BLOCK, D), w_query, w_kv, w_out, readers.T, readers.T, picks.T, fine_embed, fine_gain, coarse_gain)
+    return jnp.dot(mixed, w_out_whole, preferred_element_type=jnp.float32).astype(bf16)
 
 
 def solution(mesh):

time: 101 us -> 88.5 us (0.88)
  Pallas kernels: 96.2 us -> 83.9 us
  matrix products: 0 us -> 4.45 us
  local copies, waits for them, and re-layouts: 2.65 us -> 0 us
  other arithmetic: 1.53 us -> 0 us
    pallas_call x1, Pallas kernels: 96.2 us -> 83.9 us  [body(): pl.pallas_call(kernel, out_shape=(jax.ShapeDtypeStruct((fine_embed.shape[...]
    dot_general x0 -> x1, matrix products: none -> 4.45 us  [body(): jnp.dot(mixed, w_out_whole, preferred_element_type=jnp.float32).astype(bf16)]
    unnamed x1 -> x0, local copies, waits for them, and re-layouts: 2.65 us -> none
    reduce_sum x1 -> x0, other arithmetic: 1.53 us -> none  [body(): jnp.sum(jnp.where(readers[:, :, None] == strips, picks[:, :, None], 0), a...]
where the time goes in v3:
time: 88.5 us; the launch traced here: 88.4 us
  Pallas kernels  83.9 us (95%)
  matrix products  4.45 us (5%)
    pallas_call x1, Pallas kernels, body(): pl.pallas_call(kernel, out_shape=(jax.ShapeDtypeStruct((fine_embed.shape[...  83.9 us
    dot_general x1, matrix products, body(): jnp.dot(mixed, w_out_whole, preferred_element_type=jnp.float32).astype(bf16)  4.45 us

profile of v3, /device:TPU:1, one launch (start us, length us, event | category | flops | bytes accessed | tf_op | source)
XLA Modules:
  0.0 88.4 jit_solution(10331600349994779605)
XLA Ops:
  0.0 83.9 %shard_map.91 = (bf16[512,768]{1,0:T(8,128)(2,1)}, bf16[768,1536]{1,0:T(8,128)(2,1)}) custom-call(bf16[8,16,1536]{2,1,0:T(8,128)(2,1)} %bitcast.5, bf16[48,768]{1,0:T(8,128)(2,1)} %wq_ref.1, bf16[48,1536]{1,0:T(8,128)(2,1)} %wkv_ref.1, bf16[24,1536]{1,0:T(8,128)(2,1)} %wo_ref.1, s32[16,32]{1,0:T(8,128)} %bitcast.6, s32[16,32]{1,0:T(8,128)} %bitcast.7, ...), custom_call_target="tpu_custom_call" | custom-call | tf_op jit(solution)/shard_map/pallas_call | solution.py:396
  84.0 4.4 %convolution_convert_fusion = bf16[512,1536]{1,0:T(8,128)(2,1)} fusion(bf16[512,768]{1,0:T(8,128)(2,1)} %get-tuple-element.7, bf16[768,1536]{1,0:T(8,128)(2,1)} %get-tuple-element.8), kind=kOutput, calls=%fused_computation | convolution fusion | flops 1208745984 | bytes 4718592 | tf_op jit(solution)/shard_map/dot_general | solution.py:436

commit v4 on v3

--- a/solution.py
+++ b/solution.py
@@ -29,10 +29,10 @@
 
 
 def kernel(
-    coarse_ref, wq_ref, wkv_ref, wo_ref, readers_ref, reader_rows, pick_rows, fine_hbm, fine_gain_ref, coarse_gain_ref, mixed_hbm, w_out_hbm,
+    coarse_ref, wq_ref, wkv_ref, wo_ref, readers_ref, reader_rows, pick_rows, fine_hbm, fine_gain_ref, coarse_gain_ref, mixed, w_out,
     w_ref, x_ref, up_ref, l1, l2, l3, l4, l5, s1, s2, s3, s4, stage, far_l, far_s,
-    fine, fine_n, coarse_n, query, keyval, mixed, w_out, gains, blk_rows, blk,
-    local_sem, blk_sem, out_sem, zw_send, zw_recv, c_send, c_recv, far_send, far_recv, near_send, near_recv, up_send, up_recv,
+    fine, fine_n, coarse_n, query, keyval, gains, blk_rows, blk,
+    local_sem, blk_sem, zw_send, zw_recv, e_send, e_recv, c_send, c_recv, far_send, far_recv, near_send, near_recv, up_send, up_recv,
     a_send, a_recv, a2_send, a2_recv, b_send, b_recv, d_send, d_recv,
 ):
     img, tile = lax.axis_index("img"), lax.axis_index("tile")
@@ -59,10 +59,10 @@
 
     sibling = {"img": img, "tile": z * 2 + other}
     a_up, a_down = on_plane(a + 1, b), on_plane(a - 1, b)
-    b_up, b_down = on_plane(a, b + 1), on_plane(a, b - 1)
+    b_up, b_down, twin = on_plane(a, b + 1), on_plane(a, b - 1), on_plane(a, lax.rem(b + 2, 4))
     ahead, behind = on_z(1, core), on_z(-1, core)
 
-    partners = [sibling, a_up, a_down, b_up, b_down]
+    partners = [sibling, a_up, a_down, b_up, b_down, twin]
     partners += [on_z(j, which) for j in (-3, -2, -1, 1, 2, 3) for which in (core, other)]
     barrier = pltpu.get_barrier_semaphore()
     for partner in partners:
@@ -108,7 +108,12 @@
         copy.start()
 
     def drain():
-        whole(shards(15), zw_send, zw_recv.at[0]).wait_send()
+        for which in range(2):
+            @pl.when(kind == which)
+            def _():
+                whole(shards(7 + which), zw_send, zw_recv.at[0]).wait_send()
+                whole(shards(7 + which), e_send, e_recv.at[0]).wait_send()
+
         whole(w_ref.at[a, bp], a_send, a_recv.at[0]).wait_send()
         whole(shards(16), a2_send, a2_recv.at[0]).wait_send()
         whole(w_ref.at[:, bp, :, :, core], b_send, b_recv.at[0]).wait_send()
@@ -131,10 +136,23 @@
         return w_ref.at[a, bp, :, pl.ds(0, count), core]
 
 
+    kind = lax.rem(a // 2 + b // 2, 2)
+    onward = 1 - 2 * kind
+    next_on_z = on_z(onward, core)
+
+    def unless_last(step, which, act):
+        if step < 8:
+            act()
+        else:
+            pl.when(kind == which)(act)
+
     def zw_start(step):
-        for m in group(step):
-            where = w_ref.at[a, bp, :, along(1 - m if m <= 8 else m - 9), core]
-            go(remote(where, where, zw_send, zw_recv.at[step - 1], ahead if m <= 8 else behind))
+        where = w_ref.at[a, bp, :, along(-onward * (step - 1)), core]
+        unless_last(step, 1, remote(where, where, zw_send, zw_recv.at[step - 1], next_on_z).start)
+
+    def twin_start(step):
+        where = w_ref.at[a, bp, :, along(-onward * step), core]
+        unless_last(step, 1, remote(where, where, e_send, e_recv.at[step - 1], twin).start)
 
     def x1_start(step):
         for m in group(step):
@@ -231,22 +249,26 @@
                 ))
 
     def tick(i):
-        if i <= 8:
-            if i > 0:
-                whole(shards(len(group(i))), zw_send, zw_recv.at[i - 1]).wait_recv()
-            if i < 8:
-                zw_start(i + 1)
-            x1_start(i)
+        if 1 <= i <= 8:
+            unless_last(i, 1, whole(shards(1), zw_send, zw_recv.at[i - 1]).wait_recv)
+        if i <= 7:
+            zw_start(i + 1)
+        if 1 <= i <= 8:
+            twin_start(i)
+        if 2 <= i <= 9:
+            unless_last(i - 1, 0, whole(shards(1), e_send, e_recv.at[i - 2]).wait_recv)
         if 1 <= i <= 9:
-            whole(shards(2 * len(group(i - 1))), a_send, a_recv.at[i - 1]).wait_recv()
-            x2_start(i - 1)
+            x1_start(i - 1)
         if 2 <= i <= 10:
-            whole(shards(len(group(i - 2))), a2_send, a2_recv.at[i - 2]).wait_recv()
-            y_start(i - 2)
-        if 4 <= i <= 4 + 8:
-            count = len(group(i - 4))
-            whole(w_ref.at[:, bp, :, pl.ds(0, count), core], b_send, b_recv.at[i - 4]).wait_recv()
-            d2_start(i - 4)
+            whole(shards(2 * len(group(i - 2))), a_send, a_recv.at[i - 2]).wait_recv()
+            x2_start(i - 2)
+        if 3 <= i <= 11:
+            whole(shards(len(group(i - 3))), a2_send, a2_recv.at[i - 3]).wait_recv()
+            y_start(i - 3)
+        if 5 <= i <= 5 + 8:
+            count = len(group(i - 5))
+            whole(w_ref.at[:, bp, :, pl.ds(0, count), core], b_send, b_recv.at[i - 5]).wait_recv()
+            d2_start(i - 5)
 
     c_start(1, 0)
     tick(0)
@@ -257,19 +279,19 @@
     share_step(0)
     tick(2)
     c_pass(1, 1)
-    share_step(1)
     tick(3)
     c_pass(2, 0)
+    share_step(1)
     tick(4)
     c_pass(2, 1)
-    share_step(2)
     tick(5)
     c_pass(3, 0)
+    share_step(2)
     tick(6)
     c_pass(3, 1)
-    share_step(3)
     tick(7)
     c_pass(4, 0)
+    share_step(3)
     tick(8)
 
     for index, gain_ref in enumerate((fine_gain_ref, coarse_gain_ref)):
@@ -315,22 +337,21 @@
 
     c_pass(4, 1)
     send_far(False)
-    share_step(4)
     tick(9)
     fine_norm(0, 4)
     tick(10)
-    fine_norm(4, 8)
+    c_pass(5, 0)
     tick(11)
-    c_pass(5, 0)
     c_pass(5, 1)
     send_far(True)
+    share_step(4)
     share_step(5)
+    fine_norm(4, 8)
     tick(12)
+    tick(13)
     whole(w_ref.at[:, :, :, :, core], d_send, d_recv).wait_recv()
     project_query()
     order_out()
-    w_out_copy = pltpu.make_async_copy(w_out, w_out_hbm, out_sem.at[HEADS // 2])
-    w_out_copy.start()
     drain()
     whole(x_ref.at[0, pl.ds(0, LONG + SHORT + 1)], near_send, near_recv).wait_recv()
     whole(x_ref.at[0, pl.ds(0, 12)], far_send, far_recv).wait_recv()
@@ -346,10 +367,6 @@
     def projected(p):
         pair = jnp.concatenate([slab(6 + p), slab(12 + p)], axis=1)
         return jnp.dot(coarse_n[...], pair, preferred_element_type=jnp.float32).astype(jnp.bfloat16)
-
-    def mixed_copy(p):
-        lanes = pl.ds(pl.multiple_of(p * 128, 128), 128)
-        return pltpu.make_async_copy(mixed.at[p], mixed_hbm.at[:, lanes], out_sem.at[p])
 
     low = lax.broadcasted_iota(jnp.int32, (1, 128), 1) < HDIM
     keyval[0] = projected(0)
@@ -373,12 +390,7 @@
             exponent = jnp.exp2((scores - top) * (HDIM ** (-0.5) * LOG2E)).astype(jnp.bfloat16)
             results.append(jnp.dot(exponent, value_pair[h], preferred_element_type=jnp.float32))
         total = pltpu.roll(jnp.where(low, results[1], results[0]), HDIM, 1)
-        mixed[p] = (jnp.where(low, results[0], results[1]) / total).astype(jnp.bfloat16)
-        mixed_copy(p).start()
-
-    for p in range(HEADS // 2):
-        mixed_copy(p).wait()
-    w_out_copy.wait()
+        mixed[:, lanes] = (jnp.where(low, results[0], results[1]) / total).astype(jnp.bfloat16)
 
 
 def body(coarse, fine_embed, fine_gain, coarse_gain, w_query, w_kv, w_out, readers, picks):
@@ -396,10 +408,10 @@
     mixed, w_out_whole = pl.pallas_call(
         kernel,
         out_shape=(
-            jax.ShapeDtypeStruct((fine_embed.shape[0], HD), bf16), jax.ShapeDtypeStruct((HD, D), bf16)
+            pltpu.VMEM((fine_embed.shape[0], HD), bf16), pltpu.VMEM((HD, D), bf16)
         ),
         in_specs=[vmem] * 4 + [smem, vmem, vmem] + [hbm, vmem, vmem],
-        out_specs=(hbm, hbm),
+        out_specs=(vmem, vmem),
         scratch_shapes=[
             pltpu.VMEM((4, 2, 3, NZ, 2, 48, 128), bf16),
             pltpu.VMEM((2, NZ, BLOCK, D), bf16),
@@ -413,12 +425,11 @@
             pltpu.VMEM((256, D), bf16),
             pltpu.VMEM((512, HD), bf16),
             pltpu.VMEM((2, 256, 256), bf16),
-            pltpu.VMEM((HEADS // 2, 512, 128), bf16),
-            pltpu.VMEM((HD, D), bf16),
             pltpu.VMEM((2, 1, D), jnp.float32),
             pltpu.VMEM((NT, NT), jnp.int32),
             pltpu.SMEM((NT, NT), jnp.int32),
-            dma, dma, many(HEADS // 2 + 1),
+            dma, dma,
+            dma, many(8),
             dma, many(8),
             dma, many(2 * LONG),
             dma, dma,
@@ -430,9 +441,12 @@
             dma, dma,
         ],
         compiler_params=pltpu.CompilerParams(
-            collective_id=0, has_side_effects=True, vmem_limit_bytes=56 << 20
+            collective_id=0, has_side_effects=True, vmem_limit_bytes=40 << 20
         ),
-    )(coarse.reshape(8, BLOCK, D), w_query, w_kv, w_out, readers.T, readers.T, picks.T, fine_embed, fine_gain, coarse_gain)
+    )(*(pltpu.with_memory_space_constraint(operand, pltpu.HBM) for operand in (
+        coarse.reshape(8, BLOCK, D), w_query, w_kv, w_out, readers.T, readers.T, picks.T, fine_embed, fine_gain,
+        coarse_gain,
+    )))
     return jnp.dot(mixed, w_out_whole, preferred_element_type=jnp.float32).astype(bf16)
 
 

time: 88.5 us -> 85.3 us (0.964)
  matrix products: 4.45 us -> 2.53 us
  Pallas kernels: 83.9 us -> 82.6 us
    dot_general x1, matrix products: 4.45 us -> 2.53 us  [body(): jnp.dot(mixed, w_out_whole, preferred_element_type=jnp.float32).astype(bf16)]
    pallas_call x1, Pallas kernels: 83.9 us -> 82.6 us  [body(): pl.pallas_call(kernel, out_shape=(pltpu.VMEM((fine_embed.shape[0], HD), b...]
where the time goes in v4:
time: 85.3 us; the launch traced here: 85.2 us
  Pallas kernels  82.6 us (97%)
  matrix products  2.53 us (3%)
    pallas_call x1, Pallas kernels, body(): pl.pallas_call(kernel, out_shape=(pltpu.VMEM((fine_embed.shape[0], HD), b...  82.6 us
    dot_general x1, matrix products, body(): jnp.dot(mixed, w_out_whole, preferred_element_type=jnp.float32).astype(bf16)  2.53 us

profile of v4, /device:TPU:1, one launch (start us, length us, event | category | flops | bytes accessed | tf_op | source)
XLA Modules:
  0.0 85.2 jit_solution(8417212882518803826)
XLA Ops:
  0.0 82.6 %shard_map.91 = (bf16[512,768]{1,0:T(8,128)(2,1)S(1)}, bf16[768,1536]{1,0:T(8,128)(2,1)S(1)}) custom-call(bf16[8,16,1536]{2,1,0:T(8,128)(2,1)} %bitcast.5, bf16[48,768]{1,0:T(8,128)(2,1)} %wq_ref.1, bf16[48,1536]{1,0:T(8,128)(2,1)} %wkv_ref.1, bf16[24,1536]{1,0:T(8,128)(2,1)} %wo_ref.1, s32[16,32]{1,0:T(8,128)} %bitcast.6, s32[16,32]{1,0:T(8,128)} %bitcast.7, ...), custom_call_target="tpu_custom_call" | custom-call | tf_op jit(solution)/shard_map/pallas_call | solution.py:408
  82.7 2.5 %convolution_convert_fusion = bf16[512,1536]{1,0:T(8,128)(2,1)} fusion(bf16[512,768]{1,0:T(8,128)(2,1)S(1)} %get-tuple-element.7, bf16[768,1536]{1,0:T(8,128)(2,1)S(1)} %get-tuple-element.8), kind=kOutput, calls=%fused_computation | convolution fusion | flops 1208745984 | bytes 4718592 | tf_op jit(solution)/shard_map/dot_general | solution.py:450

commit v5 on v4

--- a/solution.py
+++ b/solution.py
@@ -68,13 +68,6 @@
     for partner in partners:
         pl.semaphore_signal(barrier, inc=1, device_id=partner, device_id_type=MESH)
 
-    for strip in range(NT):
-        blk_rows[strip : strip + 1, :] = jnp.sum(
-            jnp.where(reader_rows[...] == strip, pick_rows[...], 0), axis=0, keepdims=True
-        )
-    blk_copy = pltpu.make_async_copy(blk_rows, blk, blk_sem)
-    blk_copy.start()
-
     piece_index = 2 * a + bp
 
     @pl.when(piece_index < 2)
@@ -138,7 +131,6 @@
 
     kind = lax.rem(a // 2 + b // 2, 2)
     onward = 1 - 2 * kind
-    next_on_z = on_z(onward, core)
 
     def unless_last(step, which, act):
         if step < 8:
@@ -147,8 +139,9 @@
             pl.when(kind == which)(act)
 
     def zw_start(step):
-        where = w_ref.at[a, bp, :, along(-onward * (step - 1)), core]
-        unless_last(step, 1, remote(where, where, zw_send, zw_recv.at[step - 1], next_on_z).start)
+        stride = 1 if step == 1 else 2
+        where = w_ref.at[a, bp, :, along(-onward * (step - stride)), core]
+        unless_last(step, 1, remote(where, where, zw_send, zw_recv.at[step - 1], on_z(stride * onward, core)).start)
 
     def twin_start(step):
         where = w_ref.at[a, bp, :, along(-onward * step), core]
@@ -203,8 +196,8 @@
 
     def share(buf, steps, index, distance):
         strip = along(steps) * 2 + core
-        x_ref[core, distance] = buf[blk[strip, tile]]
-        stage[index] = buf[blk[strip, z * 2 + other]]
+        x_ref[core, distance] = normalized(buf[blk[strip, tile]].astype(jnp.float32), gains[1])
+        stage[index] = normalized(buf[blk[strip, z * 2 + other]].astype(jnp.float32), gains[1])
         go(remote(stage.at[index], x_ref.at[core, distance], near_send, near_recv, sibling))
         if abs(steps) <= 3:
             position = lax.rem(z, 4) + sign * steps
@@ -242,7 +235,7 @@
             distance = held + j if forward else NZ - held - j
             for e in range(2):
                 which = core if e == 0 else other
-                picked[2 * (j - 1) + e] = buf[blk[strip, target * 2 + which]]
+                picked[2 * (j - 1) + e] = normalized(buf[blk[strip, target * 2 + which]].astype(jnp.float32), gains[1])
                 go(remote(
                     picked.at[2 * (j - 1) + e], x_ref.at[core, distance], far_send, far_recv,
                     {"img": img, "tile": target * 2 + which},
@@ -251,8 +244,10 @@
     def tick(i):
         if 1 <= i <= 8:
             unless_last(i, 1, whole(shards(1), zw_send, zw_recv.at[i - 1]).wait_recv)
-        if i <= 7:
-            zw_start(i + 1)
+        if i == 0:
+            zw_start(1)
+        if i <= 6:
+            zw_start(i + 2)
         if 1 <= i <= 8:
             twin_start(i)
         if 2 <= i <= 9:
@@ -273,9 +268,18 @@
     c_start(1, 0)
     tick(0)
     c_start(1, 1)
-    blk_copy.wait()
+    for strip in range(NT):
+        blk_rows[strip : strip + 1, :] = jnp.sum(
+            jnp.where(reader_rows[...] == strip, pick_rows[...], 0), axis=0, keepdims=True
+        )
+    blk_copy = pltpu.make_async_copy(blk_rows, blk, blk_sem)
+    blk_copy.start()
+
     tick(1)
     c_pass(1, 0)
+    blk_copy.wait()
+    for index, gain_ref in enumerate((fine_gain_ref, coarse_gain_ref)):
+        gains[index] = gain_ref[...].reshape(1, D)
     share_step(0)
     tick(2)
     c_pass(1, 1)
@@ -294,8 +298,6 @@
     share_step(3)
     tick(8)
 
-    for index, gain_ref in enumerate((fine_gain_ref, coarse_gain_ref)):
-        gains[index] = gain_ref[...].reshape(1, D)
     fine_copy.wait()
     whole(up_ref.at[pl.ds(0, 4)], up_send, up_recv).wait_recv()
 
@@ -352,7 +354,6 @@
     whole(w_ref.at[:, :, :, :, core], d_send, d_recv).wait_recv()
     project_query()
     order_out()
-    drain()
     whole(x_ref.at[0, pl.ds(0, LONG + SHORT + 1)], near_send, near_recv).wait_recv()
     whole(x_ref.at[0, pl.ds(0, 12)], far_send, far_recv).wait_recv()
 
@@ -361,8 +362,7 @@
         reader = readers_ref[r, tile]
         lane = lax.rem(reader, 2)
         distance = lax.rem((z - reader // 2) * (1 - 2 * lane) + NZ, NZ)
-        values = x_ref[lane, distance].astype(jnp.float32)
-        coarse_n[pl.ds(pl.multiple_of(r * BLOCK, BLOCK), BLOCK), :] = normalized(values, gains[1])
+        coarse_n[pl.ds(pl.multiple_of(r * BLOCK, BLOCK), BLOCK), :] = x_ref[lane, distance]
 
     def projected(p):
         pair = jnp.concatenate([slab(6 + p), slab(12 + p)], axis=1)
@@ -371,7 +371,7 @@
     low = lax.broadcasted_iota(jnp.int32, (1, 128), 1) < HDIM
     keyval[0] = projected(0)
 
-    @pl.loop(0, HEADS // 2, unroll=2)
+    @pl.loop(0, HEADS // 2, unroll=6)
     def _(p):
         lanes = pl.ds(pl.multiple_of(p * 128, 128), 128)
         both = keyval[lax.rem(p, 2)]
@@ -391,6 +391,8 @@
             results.append(jnp.dot(exponent, value_pair[h], preferred_element_type=jnp.float32))
         total = pltpu.roll(jnp.where(low, results[1], results[0]), HDIM, 1)
         mixed[:, lanes] = (jnp.where(low, results[0], results[1]) / total).astype(jnp.bfloat16)
+
+    drain()
 
 
 def body(coarse, fine_embed, fine_gain, coarse_gain, w_query, w_kv, w_out, readers, picks):

time: 85.3 us -> 83.5 us (0.979)
  Pallas kernels: 82.6 us -> 80.4 us
    pallas_call x1, Pallas kernels: 82.6 us -> 80.4 us  [body(): pl.pallas_call(kernel, out_shape=(pltpu.VMEM((fine_embed.shape[0], HD), b...]
where the time goes in v5:
time: 83.5 us; the launch traced here: 83 us
  Pallas kernels  80.4 us (96%)
  matrix products  2.53 us (3%)
    pallas_call x1, Pallas kernels, body(): pl.pallas_call(kernel, out_shape=(pltpu.VMEM((fine_embed.shape[0], HD), b...  80.4 us
    dot_general x1, matrix products, body(): jnp.dot(mixed, w_out_whole, preferred_element_type=jnp.float32).astype(bf16)  2.53 us

profile of v5, /device:TPU:1, one launch (start us, length us, event | category | flops | bytes accessed | tf_op | source)
XLA Modules:
  0.0 83.0 jit_solution(10064630611315195028)
XLA Ops:
  0.0 80.4 %shard_map.91 = (bf16[512,768]{1,0:T(8,128)(2,1)S(1)}, bf16[768,1536]{1,0:T(8,128)(2,1)S(1)}) custom-call(bf16[8,16,1536]{2,1,0:T(8,128)(2,1)} %bitcast.5, bf16[48,768]{1,0:T(8,128)(2,1)} %wq_ref.1, bf16[48,1536]{1,0:T(8,128)(2,1)} %wkv_ref.1, bf16[24,1536]{1,0:T(8,128)(2,1)} %wo_ref.1, s32[16,32]{1,0:T(8,128)} %bitcast.6, s32[16,32]{1,0:T(8,128)} %bitcast.7, ...), custom_call_target="tpu_custom_call" | custom-call | tf_op jit(solution)/shard_map/pallas_call | solution.py:410
  80.4 2.5 %convolution_convert_fusion = bf16[512,1536]{1,0:T(8,128)(2,1)} fusion(bf16[512,768]{1,0:T(8,128)(2,1)S(1)} %get-tuple-element.7, bf16[768,1536]{1,0:T(8,128)(2,1)S(1)} %get-tuple-element.8), kind=kOutput, calls=%fused_computation | convolution fusion | flops 1208745984 | bytes 4718592 | tf_op jit(solution)/shard_map/dot_general | solution.py:452

commit v6 on v5

--- a/solution.py
+++ b/solution.py
@@ -346,11 +346,11 @@
     tick(11)
     c_pass(5, 1)
     send_far(True)
+    tick(12)
     share_step(4)
     share_step(5)
+    tick(13)
     fine_norm(4, 8)
-    tick(12)
-    tick(13)
     whole(w_ref.at[:, :, :, :, core], d_send, d_recv).wait_recv()
     project_query()
     order_out()

time: 83.5 us -> 83.5 us (level)
  no operation moved by 1% of the time
where the time goes in v6:
time: 83.5 us; the launch traced here: 83 us
  Pallas kernels  80.4 us (96%)
  matrix products  2.53 us (3%)
    pallas_call x1, Pallas kernels, body(): pl.pallas_call(kernel, out_shape=(pltpu.VMEM((fine_embed.shape[0], HD), b...  80.4 us
    dot_general x1, matrix products, body(): jnp.dot(mixed, w_out_whole, preferred_element_type=jnp.float32).astype(bf16)  2.53 us

profile of v6, /device:TPU:1, one launch (start us, length us, event | category | flops | bytes accessed | tf_op | source)
XLA Modules:
  0.0 83.0 jit_solution(12146542631259997399)
XLA Ops:
  0.0 80.4 %shard_map.91 = (bf16[512,768]{1,0:T(8,128)(2,1)S(1)}, bf16[768,1536]{1,0:T(8,128)(2,1)S(1)}) custom-call(bf16[8,16,1536]{2,1,0:T(8,128)(2,1)} %bitcast.5, bf16[48,768]{1,0:T(8,128)(2,1)} %wq_ref.1, bf16[48,1536]{1,0:T(8,128)(2,1)} %wkv_ref.1, bf16[24,1536]{1,0:T(8,128)(2,1)} %wo_ref.1, s32[16,32]{1,0:T(8,128)} %bitcast.6, s32[16,32]{1,0:T(8,128)} %bitcast.7, ...), custom_call_target="tpu_custom_call" | custom-call | tf_op jit(solution)/shard_map/pallas_call | solution.py:410
  80.4 2.5 %convolution_convert_fusion = bf16[512,1536]{1,0:T(8,128)(2,1)} fusion(bf16[512,768]{1,0:T(8,128)(2,1)S(1)} %get-tuple-element.7, bf16[768,1536]{1,0:T(8,128)(2,1)S(1)} %get-tuple-element.8), kind=kOutput, calls=%fused_computation | convolution fusion | flops 1208745984 | bytes 4718592 | tf_op jit(solution)/shard_map/dot_general | solution.py:452
